TPU v7x, 32 devices: a whole 2x2x4 slice. The times are simulated.
32 devices in a mesh: samp: 8 (over z, x), chan: 4 (over y, core).
Axes of the slice: x: 2, y: 2, z: 4, core: 2. Of those that a mesh axis runs over, the one named last changes fastest.
Arguments:
- loads: float32 [256, 24576], P('chan', 'samp')
- coords: float32 [6, 24576], P(None, 'samp'), may hold values from -6 to 6
- coreg_factor: float32 [256, 256], P('chan'), may hold values from -0.375 to 0.375
- noise: float32 [256], P('chan'), may hold values from 0.1 to 1
- run_perm: int32 [24576], P('samp'), may hold values from 0 to 24575, as said below
- block_nbrs: int32 [192, 12], P('samp'), may hold values from 0 to 191, as said below
- nbr_count: int32 [192], P('samp'), may hold values from 1 to 12, as said below
Outputs:
- solution: float32 [256, 24576], P('chan', 'samp')
- residual: float32 [256, 24576], P('chan', 'samp')
Inputs may be any that keep to these rules, and one draw needn't show every extreme that they name: `block_nbrs`: the blocks are cut into clusters of consecutive blocks, each of 1 to 12 blocks. Row b lists the blocks of b's cluster in increasing order in its first nbr_count[b] entries; its other entries hold b itself. `nbr_count`: the size of block b's cluster; some block's cluster has 12 blocks. `run_perm`: within each aligned range of 3072 positions (the runs of one samp device), a permutation of that range.
All inputs are finite; a program needn't handle non-finite values.
Results may differ from a plain program's by a relative error of at most 0.0035.
Values may be sent and summed in bfloat16 or wider, within the bound.
A program may use at most 64 MiB of HBM per device.

v0:
```python
import jax
import jax.numpy as jnp
from jax import lax
from jax.sharding import PartitionSpec as P

ITERS = 2


SUPPORT = 5.0
AMPLITUDE = 0.05


def extended(block, sides, width):
    for axis, dim in sides:
        count = lax.axis_size(axis)
        forward = [(i, i + 1) for i in range(count - 1)]
        backward = [(target, source) for source, target in forward]
        low = lax.ppermute(
            lax.slice_in_dim(block, block.shape[dim] - width, None, axis=dim), axis, forward
        )
        high = lax.ppermute(lax.slice_in_dim(block, 0, width, axis=dim), axis, backward)
        block = jnp.concatenate([low, block, high], axis=dim)
    return block


def wendland(squared):
    radius_frac = jnp.sqrt(squared) / SUPPORT
    remain = jnp.maximum(1.0 - radius_frac, 0.0)
    cubed = remain * remain * remain
    return cubed * cubed * (6.0 * radius_frac + 1.0)


def squared_norm(remainder):
    return lax.psum(jnp.sum(remainder * remainder), ("samp", "chan"))


def per_device(loads, coords, coreg_factor, noise, run_perm, block_nbrs, nbr_count):
    chan_local, runs_local = loads.shape
    blocks_local = nbr_count.shape[0]
    block_runs = runs_local // blocks_local
    dims = coords.shape[0]
    slot_limit = block_nbrs.shape[1]
    device_pos = lax.axis_index("samp")
    local_perm = run_perm - device_pos * runs_local
    sorted_coords = jnp.take(coords, local_perm, axis=1)
    sorted_loads = jnp.take(loads, local_perm, axis=1)
    full_factor = lax.all_gather(coreg_factor, "chan", axis=0, tiled=True)
    reach_runs = blocks_local * block_runs
    window_blocks = blocks_local + 2 * blocks_local
    widened_coords = extended(sorted_coords, (("samp", 1),), reach_runs)
    coord_blocks = widened_coords.reshape(dims, window_blocks, block_runs)
    own_coords = sorted_coords.reshape(dims, blocks_local, block_runs)
    nbr_local = block_nbrs - (device_pos * blocks_local - blocks_local)
    slot_total = jnp.max(nbr_count)

    def build_tile(slot_index):
        partner_ids = lax.dynamic_index_in_dim(nbr_local, slot_index, 1, keepdims=False)
        live_mask = (slot_index < nbr_count).astype(jnp.float32)
        partner = jnp.take(coord_blocks, partner_ids, axis=1)
        squared = jnp.zeros((blocks_local, block_runs, block_runs), jnp.float32)
        for component in range(dims):
            difference = own_coords[component][:, :, None] - partner[component][:, None, :]
            squared = squared + difference * difference
        return (wendland(squared) * live_mask[:, None, None]).astype(jnp.bfloat16)

    all_tiles = lax.map(build_tile, jnp.arange(slot_limit, dtype=jnp.int32))
    iterate = jnp.zeros_like(sorted_loads)
    remainder = sorted_loads
    direction = sorted_loads
    norm_now = squared_norm(remainder)
    for iteration in range(ITERS):
        rounded = direction.astype(jnp.bfloat16)
        coreg_cols = jnp.dot(full_factor, coreg_factor.T, precision=lax.Precision.HIGHEST)
        rounded_wide = rounded.astype(jnp.float32)
        mixed = lax.psum_scatter(
            jnp.dot(coreg_cols, rounded_wide, precision=lax.Precision.HIGHEST),
            "chan",
            scatter_dimension=0,
            tiled=True,
        )
        mixed_b = mixed.astype(jnp.bfloat16)
        widened = extended(mixed_b, (("samp", 1),), reach_runs)
        value_blocks = widened.reshape(chan_local, window_blocks, block_runs)

        def slot_step(slot_index, summed):
            partner_ids = lax.dynamic_index_in_dim(nbr_local, slot_index, 1, keepdims=False)
            kernel_tile = lax.dynamic_index_in_dim(all_tiles, slot_index, 0, keepdims=False)
            partner_vals = jnp.take(value_blocks, partner_ids, axis=1)
            return summed + jnp.einsum(
                "bim,cbm->cbi", kernel_tile, partner_vals, preferred_element_type=jnp.float32
            )

        summed = lax.fori_loop(
            0, slot_total, slot_step, jnp.zeros((chan_local, blocks_local, block_runs), jnp.float32)
        )
        mapped = AMPLITUDE * summed.reshape(chan_local, runs_local) + noise[:, None] * direction
        step_size = norm_now / lax.psum(jnp.sum(direction * mapped), ("samp", "chan"))
        iterate = iterate + step_size * direction
        remainder = remainder - step_size * mapped
        if iteration + 1 < ITERS:
            norm_next = squared_norm(remainder)
            direction = remainder + norm_next / norm_now * direction
            norm_now = norm_next
    solution = jnp.zeros_like(iterate).at[:, local_perm].set(iterate)
    residual = jnp.zeros_like(remainder).at[:, local_perm].set(remainder)
    return (solution, residual)


def solution(mesh):
    return jax.shard_map(
        per_device,
        mesh=mesh,
        in_specs=(
            P("chan", "samp"),
            P(None, "samp"),
            P("chan", None),
            P("chan"),
            P("samp"),
            P("samp", None),
            P("samp"),
        ),
        out_specs=(P("chan", "samp"), P("chan", "samp")),
        check_vma=False,
    )
```

profile of v0, /device:TPU:0, one launch (start us, length us, event | category | flops | bytes accessed | tf_op | source)
XLA Modules:
  0.0 558.0 jit_solution(15772431287520296315)
XLA Ops:
  9.6 7.2 %all_gather.3 = f32[256,256]{1,0:T(8,128)S(1)} all-gather(f32[64,256]{1,0:T(8,128)S(1)} %copy-done.6), channel_id=1, replica_groups=mesh['samp'=8,'chan'=4] {'chan'}, dimensions={0}, use_global_device_ids=true | all-gather | bytes 327680 | tf_op jit(solution)/shard_map/all_gather | solution.py:47
  17.2 8.1 %gather_fusion.3 = f32[3072,64]{1,0:T(8,128)S(1)} fusion(f32[64,3072]{0,1:T(8,128)S(1)} %copy.31, s32[3072]{0:T(1024)S(1)} %broadcast_clamp_fusion), kind=kCustom, calls=%fused_computation.3 | custom fusion | bytes 1585152 | tf_op jit(solution)/shard_map/jit(_take)/gather | solution.py:46
  32.0 9.5 %gather_fusion.4 = f32[3072,6]{1,0:T(8,128)S(1)} fusion(f32[6,3072]{0,1:T(8,128)} %copy.33, s32[3072]{0:T(1024)S(1)} %broadcast_clamp_fusion), kind=kCustom, calls=%fused_computation.4 | custom fusion | bytes 159744 | tf_op jit(solution)/shard_map/jit(_take)/gather | solution.py:45
  56.0 12.8 %reduce-scatter.3.cloned.1.call-done = f32[64,3072]{1,0:T(8,128)} async-done(((f32[256,3072]{1,0:T(8,128)}), f32[64,3072]{1,0:T(8,128)}) %reduce-scatter.3.cloned.1.call-update) | async-done | bytes 786448 | tf_op jit(solution)/shard_map/reduce_scatter | solution.py:75
  75.5 111.9 %while.32 = (s32[]{:T(128)}, bf16[12,24,128,128]{3,2,1,0:T(8,128)(2,1)}, f32[6,24,128]{2,1,0:T(8,128)S(1)}, s32[12]{0:T(128)S(1)}, s32[24,12]{0,1:T(8,128)}, /*i...) while((s32[]{:T(128)}, bf16[12,24,128,128]{3,2,1,0:T(8,128)(2,1)}, ...), condition=%wide.region_4.5_spmd, body=%wide.region_3.4_spmd.sunk | while | flops 11029701 | bytes 1529195 | solution.py:66
  89.4 4.7 fusion.63
  98.8 4.7 fusion.63
  108.1 4.7 fusion.63
  126.7 4.7 fusion.63
  136.1 4.7 fusion.63
  145.4 4.7 fusion.63
  154.7 4.7 fusion.63
  164.0 4.7 fusion.63
  173.4 4.7 fusion.63
  182.7 4.7 fusion.63
  189.9 61.9 %while.33 = (s32[]{:T(128)}, f32[64,24,128]{2,0,1:T(8,128)S(1)}, s32[]{:T(128)}, s32[24,12]{0,1:T(8,128)}, bf16[64,72,128]{2,0,1:T(8,128)(2,1)}, /*index=5*/bf16...) while((s32[]{:T(128)}, f32[64,24,128]{2,0,1:T(8,128)S(1)}, s32[]{:T(128)}, s32[24,12]{0,1:T(8,128)}, ...), condition=%wide.region_7.9_spmd, body=%wide.region_6.8_spmd.sunk | while | flops 50726036 | bytes 3543607 | solution.py:93
  252.8 40.7 %all-reduce = (f32[]{:T(128)}, f32[]{:T(128)}) all-reduce(f32[]{:T(128)} %multiply_reduce_fusion, f32[]{:T(128)} %multiply_reduce_fusion.3), channel_id=1, replica_groups=mesh['samp'=8,'chan'=4] {'samp','chan'}, use_global_device_ids=true, to_apply=%region_1.2 | all-reduce | flops 2 | bytes 16 | tf_op jit(solution)/shard_map/psum | solution.py:34
  296.7 41.6 %psum.30 = f32[]{:T(128)} all-reduce(f32[]{:T(128)} %get-tuple-element.274), channel_id=1, replica_groups=mesh['samp'=8,'chan'=4] {'samp','chan'}, use_global_device_ids=true, to_apply=%region_11.13 | all-reduce | flops 1 | bytes 8 | tf_op jit(solution)/shard_map/psum | solution.py:34
  349.5 38.2 %reduce-scatter.5.cloned.1.call-done = f32[64,3072]{1,0:T(8,128)} async-done(((f32[256,3072]{1,0:T(8,128)}), f32[64,3072]{1,0:T(8,128)}) %reduce-scatter.5.cloned.1.call-update) | async-done | bytes 786448 | tf_op jit(solution)/shard_map/reduce_scatter | solution.py:75
  393.6 15.5 %collective-permute-done.4 = bf16[64,3072]{1,0:T(8,128)(2,1)S(1)} collective-permute-done((bf16[64,3072]{1,0:T(8,128)(2,1)S(1)}, bf16[64,3072]{1,0:T(8,128)(2,1)S(1)}, u32[]{:S(2)}, u32[]{:S(2)}) %collective-permute-start.4) | collective-permute-done | bytes 393248 | tf_op jit(solution)/shard_map/ppermute | solution.py:18
  410.4 61.9 %while.34 = (s32[]{:T(128)}, f32[64,24,128]{2,0,1:T(8,128)S(1)}, s32[]{:T(128)}, s32[24,12]{0,1:T(8,128)}, bf16[64,72,128]{2,0,1:T(8,128)(2,1)}, /*index=5*/bf16...) while((s32[]{:T(128)}, f32[64,24,128]{2,0,1:T(8,128)S(1)}, s32[]{:T(128)}, ...), condition=%wide.region_14.16_spmd, body=%wide.region_13.15_spmd.sunk | while | flops 50726036 | bytes 3543607 | solution.py:93
  478.3 41.3 %psum.31 = f32[]{:T(128)} all-reduce(f32[]{:T(128)} %get-tuple-element.273), channel_id=1, replica_groups=mesh['samp'=8,'chan'=4] {'samp','chan'}, use_global_device_ids=true, to_apply=%region_16.18 | all-reduce | flops 1 | bytes 8 | tf_op jit(solution)/shard_map/psum | solution.py:97
  524.6 9.8 %scatter_custom_fusion.1 = f32[64,3072]{0,1:T(8,128)} fusion(s32[3072]{0:T(1024)} %copy-done.8, f32[64,3072]{0,1:T(8,128)} %fusion.26, f32[]{:T(128)} %constant.140.clone.1), kind=kCustom, calls=%fused_computation.50 | custom fusion | bytes 2359808 | tf_op jit(solution)/shard_map/scatter | solution.py:105
  537.2 11.2 %scatter_custom_fusion = f32[64,3072]{0,1:T(8,128)} fusion(s32[3072]{0:T(1024)} %copy-done.8, f32[64,3072]{0,1:T(8,128)S(1)} %copy-done.2, f32[3072,64]{1,0:T(8,128)S(1)} %gather_fusion.3, f32[]{:T(128)S(6)} %div.14, f32[]{:T(128)S(6)} %div.12, f32[]{:T(128)} %constant.146.clone.1, f32[]{:T(128)} %constant.140.clone.1, ...), kind=kCustom, calls=%fused_computation.55 | custom fusion | flops 786432 | bytes 2363400 | tf_op jit(solution)/shard_map/scatter | solution.py:104
  (266 shorter events, 216.7 us)
Async XLA Ops:
  7.2 2.4 copy-start.6
  7.2 61.7 %reduce-scatter.3.cloned.1.call-start = ((), (), s32[]{:S(2)}) async-start(), calls=%async_computation.2 | async-start | bytes 3932160 | tf_op jit(solution)/shard_map/reduce_scatter | solution.py:75
  7.9 17.4 %copy-start.8 = (s32[3072]{0:T(1024)}, s32[3072]{0:T(1024)S(1)}, u32[]{:S(2)}) copy-start(s32[3072]{0:T(1024)S(1)} %get-tuple-element.259) | copy-start | bytes 36868
  17.2 8.1 %copy-start.4 = (f32[256,64]{0,1:T(8,128)}, f32[256,64]{0,1:T(8,128)S(1)}, u32[]{:S(2)}) copy-start(f32[256,64]{0,1:T(8,128)S(1)} %fusion.49) | copy-start | bytes 196612
  29.4 0.9 copy-start.7
  29.5 358.2 %reduce-scatter.5.cloned.1.call-start = ((), (), s32[]{:S(2)}) async-start(), calls=%async_computation.3 | async-start | bytes 3932160 | tf_op jit(solution)/shard_map/reduce_scatter | solution.py:75
  44.0 7.1 %copy-start.10 = (s32[24,12]{0,1:T(8,128)S(1)}, s32[24,12]{0,1:T(8,128)}, u32[]{:S(2)}) copy-start(s32[24,12]{0,1:T(8,128)} %param.20) | copy-start | bytes 3460
  45.9 9.4 %collective-permute-start.2 = (f32[6,3072]{1,0:T(8,128)S(1)}, f32[6,3072]{1,0:T(8,128)S(1)}, u32[]{:S(2)}, u32[]{:S(2)}) collective-permute-start(f32[6,3072]{1,0:T(8,128)S(1)} %copy.35), channel_id=1, source_target_pairs={{0,4},{4,8},{8,12},{12,16},{16,20},{20,24},{24,28},{1,5},{5,9},{9,... | collective-permute-start | bytes 221192 | tf_op jit(solution)/shard_map/ppermute | solution.py:18
  49.3 6.7 %collective-permute-start.3 = (f32[6,3072]{1,0:T(8,128)S(1)}, f32[6,3072]{1,0:T(8,128)S(1)}, u32[]{:S(2)}, u32[]{:S(2)}) collective-permute-start(f32[6,3072]{1,0:T(8,128)S(1)} %copy.35), channel_id=1, source_target_pairs={{4,0},{8,4},{12,8},{16,12},{20,16},{24,20},{28,24},{5,1},{9,5},{13... | collective-permute-start | bytes 221192 | tf_op jit(solution)/shard_map/ppermute | solution.py:21
  53.9 0.7 copy-start.11
  54.6 240.3 %copy-start.3 = (f32[64,24,128]{2,0,1:T(8,128)}, f32[64,24,128]{2,0,1:T(8,128)S(1)}, u32[]{:S(2)}) copy-start(f32[64,24,128]{2,0,1:T(8,128)S(1)} %copy.32) | copy-start | bytes 2359300
  70.0 117.4 %collective-permute-start = (bf16[64,3072]{1,0:T(8,128)(2,1)S(1)}, bf16[64,3072]{1,0:T(8,128)(2,1)}, u32[]{:S(2)}, u32[]{:S(2)}) collective-permute-start(bf16[64,3072]{1,0:T(8,128)(2,1)S(1)} %convert_element_type.38), channel_id=1, source_target_pairs={{0,4},{4,8},{8,12},{12,16},{16,20},{20,24},{24,28},{1,5},{5,9},{9,... | collective-permute-start | bytes 1179656 | tf_op jit(solution)/shard_map/ppermute | solution.py:18
  74.2 113.2 %collective-permute-start.1 = (bf16[64,3072]{1,0:T(8,128)(2,1)S(1)}, bf16[64,3072]{1,0:T(8,128)(2,1)}, u32[]{:S(2)}, u32[]{:S(2)}) collective-permute-start(bf16[64,3072]{1,0:T(8,128)(2,1)S(1)} %convert_element_type.38), channel_id=1, source_target_pairs={{4,0},{8,4},{12,8},{16,12},{20,16},{24,20},{28,24},{5,1},{9,5},{13... | collective-permute-start | bytes 1179656 | tf_op jit(solution)/shard_map/ppermute | solution.py:21
  189.9 61.9 %copy-start.9 = (f32[64]{0:T(128)S(1)}, f32[64]{0:T(128)}, u32[]{:S(2)}) copy-start(f32[64]{0:T(128)} %param.18) | copy-start | bytes 772
  342.4 4.0 copy-start.5
  345.1 1.2 copy-start.1
  388.9 20.2 %collective-permute-start.4 = (bf16[64,3072]{1,0:T(8,128)(2,1)S(1)}, bf16[64,3072]{1,0:T(8,128)(2,1)S(1)}, u32[]{:S(2)}, u32[]{:S(2)}) collective-permute-start(bf16[64,3072]{1,0:T(8,128)(2,1)S(1)} %convert_element_type.40), channel_id=1, source_target_pairs={{0,4},{4,8},{8,12},{12,16},{16,20},{20,24},{24,28},{1,5},{5,9},{9,... | collective-permute-start | bytes 1179656 | tf_op jit(solution)/shard_map/ppermute | solution.py:18
  392.3 16.8 %collective-permute-start.5 = (bf16[64,3072]{1,0:T(8,128)(2,1)S(1)}, bf16[64,3072]{1,0:T(8,128)(2,1)S(1)}, u32[]{:S(2)}, u32[]{:S(2)}) collective-permute-start(bf16[64,3072]{1,0:T(8,128)(2,1)S(1)} %convert_element_type.40), channel_id=1, source_target_pairs={{4,0},{8,4},{12,8},{16,12},{20,16},{24,20},{28,24},{5,1},{9,5},{13... | collective-permute-start | bytes 1179656 | tf_op jit(solution)/shard_map/ppermute | solution.py:21
  475.4 45.5 %copy-start = (f32[64,24,128]{0,2,1:T(8,128)S(1)}, f32[64,24,128]{0,2,1:T(8,128)}, u32[]{:S(2)}) copy-start(f32[64,24,128]{0,2,1:T(8,128)} %copy.40) | copy-start | bytes 2359300
  534.4 2.9 copy-start.2
Sparse Core Ops, SparseCore 0:
  29.6 39.2 reduce-scatter.2
  349.6 38.0 reduce-scatter.4
where the time goes:
time: 563 us; the launch traced here: 558 us
  blocking collectives  131 us (23%)
  other arithmetic  127 us (23%)
  local copies, waits for them, and re-layouts  108 us (19%)
  waiting for transfers between devices  67.2 us (12%)
  matrix products  52.5 us (9%)
  loops' own time  40.1 us (7%)
  between operations  18.3 us (3%)
  starting transfers between devices  14.9 us (3%)
    psum x2, blocking collectives, squared_norm(): return lax.psum(jnp.sum(remainder * remainder), ('samp', 'chan'))  82.3 us
    dynamic_update_slice x12, other arithmetic, per_device(): all_tiles = lax.map(build_tile, jnp.arange(slot_limit, dtype=jnp.int32))  56.4 us
    reduce_scatter x2, waiting for transfers between devices, per_device(): lax.psum_scatter(jnp.dot(coreg_cols, rounded_wide, precision=lax.Precisio...  51 us
    gather x24, local copies, waits for them, and re-layouts, slot_step(): partner_vals = jnp.take(value_blocks, partner_ids, axis=1)  45.4 us
    dot_general x24, matrix products, slot_step(): jnp.einsum('bim,cbm->cbi', kernel_tile, partner_vals, preferred_element_t...  44.9 us
    psum x1, blocking collectives, per_device(): lax.psum(jnp.sum(direction * mapped), ('samp', 'chan'))  41.3 us
    another operation x1, loops' own time, per_device(): all_tiles = lax.map(build_tile, jnp.arange(slot_limit, dtype=jnp.int32))  23.4 us
    and x24, other arithmetic, slot_step(): partner_vals = jnp.take(value_blocks, partner_ids, axis=1)  16.7 us
  transfers between devices with their start and end apart: 8, of which 4 were waited for; matrix products, arithmetic and copies ran while one was open for 19% of the time, Pallas kernels for 0%

commit v1 on v0

v1 whole, which is shorter than its diff:
```python
import functools

import jax
import jax.numpy as jnp
from jax import lax
from jax.experimental import pallas as pl
from jax.experimental.pallas import tpu as pltpu
from jax.sharding import PartitionSpec as P

SUPPORT = 5.0
AMPLITUDE = 0.05
LANES = 128
CHUNKS = 4
MESH = pl.DeviceIdType.MESH
F32 = jnp.float32
BF16 = jnp.bfloat16


def lane_tile(index):
    return pl.ds(pl.multiple_of(index * LANES, LANES), LANES)


def permute_tiles(source, order, target, begin, end):
    rows, columns = source.shape

    def step(tile, carry):
        index = order[pl.ds(tile, 1), :]
        lane = jnp.broadcast_to(index % LANES, (rows, LANES))
        origin = jnp.broadcast_to(index // LANES, (rows, LANES))
        result = jnp.zeros((rows, LANES), F32)
        for part in range(columns // LANES):
            picked = jnp.take_along_axis(
                source[:, part * LANES : (part + 1) * LANES], lane, axis=1, mode="promise_in_bounds"
            )
            result = jnp.where(origin == part, picked, result)
        target[:, lane_tile(tile)] = result
        return carry

    lax.fori_loop(begin, end, step, 0)


def pieces(value):
    high = value.astype(BF16).astype(F32)
    rest = value - high
    middle = rest.astype(BF16).astype(F32)
    return high, middle, (rest - middle).astype(BF16).astype(F32)


def fold(value):
    total = value[0:8]
    for row in range(8, value.shape[0], 8):
        total = total + value[row : row + 8]
    return total


def whole_sum(value):
    return jnp.sum(jnp.sum(value, axis=0, keepdims=True), axis=1, keepdims=True)


def sorter(blocks, loads, coords, perm, sorted_loads, sorted_coords, order, coords_in):
    order[...] = perm[...] - lax.axis_index("samp") * loads.shape[1]
    coords_in[...] = jnp.zeros_like(coords_in)
    coords_in[0 : coords.shape[0], :] = coords[...] * (1.0 / SUPPORT)
    permute_tiles(coords_in, order, sorted_coords, 0, blocks)
    permute_tiles(loads, order, sorted_loads, 0, blocks)


def unsorter(blocks, sorted_sol, sorted_res, inverse, sol, res, order):
    order[...] = inverse[...].astype(jnp.int32)
    permute_tiles(sorted_sol, order, sol, 0, blocks)
    permute_tiles(sorted_res, order, res, 0, blocks)


def solver(
    samp_count, blocks, slots,
    sorted_loads, sorted_coords, factor, noise, perm, counts, first_block,
    sol, res, inverse,
    inv_sum, coords_ext, own_terms, ext_terms, tiles,
    factors, coreg, direction, image, gathered, values_first, values_second,
    red_chan, red_samp,
    fac_send, fac_recv, gat_send, gat_recv, halo_send, halo_recv,
    rc_send, rc_recv, rs_send, rs_recv,
):
    rows, runs = sorted_loads.shape
    halo = (slots - 1) * LANES
    extent = runs + 2 * halo
    edge = slots - 1
    widened = blocks + 2 * edge
    values = (values_first, values_second)
    chunk = runs // CHUNKS
    samp = lax.axis_index("samp")
    chan = lax.axis_index("chan")
    core_peer = chan + 1 - 2 * (chan % 2)
    far_peer = (chan + 2) % 4
    chan_peers = (core_peer, far_peer, 3 - chan)

    barrier = pltpu.get_barrier_semaphore()
    for peer in chan_peers:
        pl.semaphore_signal(barrier, inc=1, device_id={"chan": peer}, device_id_type=MESH)

    def greet(hop, carry):
        pl.semaphore_signal(
            barrier, inc=1, device_id={"samp": (samp + hop) % samp_count}, device_id_type=MESH
        )
        return carry

    lax.fori_loop(1, samp_count, greet, 0)

    coords_ext[:, halo : halo + runs] = sorted_coords[...]

    @pl.when(samp == 0)
    def _():
        coords_ext[:, 0:halo] = jnp.zeros((8, halo), F32)
        for turn in range(2):
            values[turn][0:edge] = jnp.zeros((edge, rows, LANES), BF16)

    @pl.when(samp == samp_count - 1)
    def _():
        coords_ext[:, extent - halo : extent] = jnp.zeros((8, halo), F32)
        for turn in range(2):
            values[turn][widened - edge : widened] = jnp.zeros((edge, rows, LANES), BF16)

    factors[chan] = factor[...]
    pl.semaphore_wait(barrier, 3 + samp_count - 1)

    def halo_copies(regions, turn):
        own_low, own_high, low, high = regions
        to_low = pltpu.make_async_remote_copy(
            src_ref=own_low,
            dst_ref=high,
            send_sem=halo_send.at[turn, 0],
            recv_sem=halo_recv.at[turn, 0],
            device_id={"samp": (samp + samp_count - 1) % samp_count},
            device_id_type=MESH,
        )
        to_high = pltpu.make_async_remote_copy(
            src_ref=own_high,
            dst_ref=low,
            send_sem=halo_send.at[turn, 1],
            recv_sem=halo_recv.at[turn, 1],
            device_id={"samp": (samp + 1) % samp_count},
            device_id_type=MESH,
        )
        return to_low, to_high

    def halo_start_low(copies):
        @pl.when(samp > 0)
        def _():
            copies[0].start()

    def halo_start_high(copies):
        @pl.when(samp < samp_count - 1)
        def _():
            copies[1].start()

    def halo_wait(copies):
        @pl.when(samp > 0)
        def _():
            copies[0].wait_send()
            copies[1].wait_recv()

        @pl.when(samp < samp_count - 1)
        def _():
            copies[1].wait_send()
            copies[0].wait_recv()

    coord_copies = halo_copies(
        [coords_ext.at[:, pl.ds(first, halo)] for first in (halo, runs, 0, extent - halo)], 0
    )
    halo_start_low(coord_copies)
    halo_start_high(coord_copies)

    factor_copies = []
    for relation, peer in enumerate(chan_peers):
        factor_copies.append(
            pltpu.make_async_remote_copy(
                src_ref=factors.at[chan],
                dst_ref=factors.at[chan],
                send_sem=fac_send.at[relation],
                recv_sem=fac_recv.at[relation],
                device_id={"chan": peer},
                device_id_type=MESH,
            )
        )
        factor_copies[-1].start()

    def gather_copy(turn, kind, part, owner, peer):
        place = gathered.at[turn, owner, :, pl.ds(part * chunk, chunk)]
        return pltpu.make_async_remote_copy(
            src_ref=place,
            dst_ref=place,
            send_sem=gat_send.at[turn, kind, part],
            recv_sem=gat_recv.at[turn, kind, part],
            device_id={"chan": peer},
            device_id_type=MESH,
        )

    def gather_start(turn, part):
        gather_copy(turn, 1, part, chan, far_peer).start()
        gather_copy(turn, 0, part, chan, core_peer).start()

    def gather_forward(turn, part):
        gather_copy(turn, 1, part, far_peer, far_peer).wait_recv()
        gather_copy(turn, 2, part, far_peer, core_peer).start()

    def gather_finish(turn):
        for part in range(CHUNKS):
            gather_copy(turn, 0, part, chan, core_peer).wait_send()
            gather_copy(turn, 1, part, chan, far_peer).wait_send()
            gather_copy(turn, 2, part, far_peer, core_peer).wait_send()
            gather_copy(turn, 0, part, core_peer, core_peer).wait_recv()
            gather_copy(turn, 2, part, 3 - chan, core_peer).wait_recv()

    per_chunk = blocks // CHUNKS
    for part in range(CHUNKS):
        columns = pl.ds(part * chunk, chunk)
        gathered[0, chan, :, columns] = sorted_loads[:, columns].astype(BF16)
        gather_start(0, part)

    row_id = lax.broadcasted_iota(jnp.int32, (8, LANES), 0)

    def own_step(tile, carry):
        point = sorted_coords[:, lane_tile(tile)]
        norm = jnp.sum(point * point, axis=0, keepdims=True)
        terms = jnp.where(row_id == 6, 1.0, jnp.where(row_id == 7, norm, -2.0 * point))
        high, middle, low = pieces(terms)
        stacked = jnp.concatenate(
            [high, middle, high, middle, low, high, jnp.zeros((LANES - 48, LANES), F32)], axis=0
        )
        own_terms[:, lane_tile(tile)] = stacked.astype(BF16)
        return carry

    lax.fori_loop(0, blocks, own_step, 0)
    halo_wait(coord_copies)

    def ext_step(tile, carry):
        point = coords_ext[:, lane_tile(tile)]
        norm = jnp.sum(point * point, axis=0, keepdims=True)
        terms = jnp.where(row_id == 6, norm, jnp.where(row_id == 7, 1.0, point))
        high, middle, low = pieces(terms)
        stacked = jnp.concatenate(
            [high, high, middle, middle, high, low, jnp.zeros((LANES - 48, LANES), F32)], axis=0
        )
        ext_terms[tile] = stacked.T.astype(BF16)
        return carry

    lax.fori_loop(0, extent // LANES, ext_step, 0)

    def window_start(block):
        return first_block[block]

    def tile_step(block, carry):
        start = window_start(block)
        count = counts[pl.ds(block, 1), :]
        own = own_terms[:, lane_tile(block)]
        for slot in range(slots):
            partner = ext_terms[start + slot]
            squared = jnp.dot(partner, own, preferred_element_type=F32)
            squared = jnp.maximum(squared, 1e-20)
            radius = squared * lax.rsqrt(squared)
            live = jnp.where(count > slot, 1.0, 0.0)
            remain = jnp.maximum(live - radius, 0.0)
            cubed = remain * remain * remain
            tile = cubed * cubed * (6.0 * radius + 1.0)
            tiles[block, slot * LANES : (slot + 1) * LANES, :] = tile.astype(BF16)
        return carry

    first_part = (blocks * 5) // 8
    lax.fori_loop(0, first_part, tile_step, 0)
    for part in range(CHUNKS):
        gather_forward(0, part)
    lax.fori_loop(first_part, blocks, tile_step, 0)

    for copy in factor_copies:
        copy.wait()
    coreg_rows = lax.dot_general(
        factor[...],
        factors[...].reshape(4 * rows, factor.shape[1]),
        (((1,), (1,)), ((), ())),
        precision=lax.Precision.HIGHEST,
        preferred_element_type=F32,
    )
    for number, piece in enumerate(pieces(coreg_rows)):
        coreg[number * rows : (number + 1) * rows, :] = piece.astype(BF16)

    def mix(turn, begin, end):
        weights = coreg[...]
        while begin < end:
            width = min(2 * LANES, end - begin)
            operand = gathered[turn, :, :, begin : begin + width].reshape(4 * rows, width)
            product = jnp.dot(weights, operand, preferred_element_type=F32)
            mixed = product[0:rows] + product[rows : 2 * rows] + product[2 * rows : 3 * rows]
            for part in range(width // LANES):
                values[turn][edge + begin // LANES + part] = mixed[
                    :, part * LANES : (part + 1) * LANES
                ].astype(BF16)
            begin += width

    def exchange(turn):
        copies = halo_copies(
            [
                values[turn].at[pl.ds(first, edge)]
                for first in (edge, blocks, 0, widened - edge)
            ],
            turn + 1,
        )
        mix(turn, 0, halo)
        halo_start_low(copies)
        if runs - halo >= halo:
            mix(turn, runs - halo, runs)
            halo_start_high(copies)
            mix(turn, halo, runs - halo)
        halo_wait(copies)

    noise_wide = jnp.broadcast_to(noise[...], (rows, LANES))
    nothing = jnp.zeros((rows, LANES), F32)

    def apply_block(turn, block, operand):
        start = window_start(block)
        partner = jnp.concatenate([values[turn][start + slot] for slot in range(slots)], axis=1)
        summed = jnp.dot(partner, tiles[block], preferred_element_type=F32)
        return AMPLITUDE * summed + noise_wide * operand

    def reduce_chan_copy(turn, relation, owner, peer):
        return pltpu.make_async_remote_copy(
            src_ref=red_chan.at[turn, owner],
            dst_ref=red_chan.at[turn, owner],
            send_sem=rc_send.at[turn, relation],
            recv_sem=rc_recv.at[turn, relation],
            device_id={"chan": peer},
            device_id_type=MESH,
        )

    def reduce_begin(turn, parts):
        for number, part in enumerate(parts):
            red_chan[turn, chan, number * 8 : (number + 1) * 8, :] = fold(part)
        for number in range(len(parts), 3):
            red_chan[turn, chan, number * 8 : (number + 1) * 8, :] = jnp.zeros((8, LANES), F32)
        for relation, peer in enumerate(chan_peers):
            reduce_chan_copy(turn, relation, chan, peer).start()

    def reduce_samp_copy(turn, hop, owner):
        return pltpu.make_async_remote_copy(
            src_ref=red_samp.at[turn, owner],
            dst_ref=red_samp.at[turn, owner],
            send_sem=rs_send.at[turn, hop],
            recv_sem=rs_recv.at[turn, owner],
            device_id={"samp": (samp + hop) % samp_count},
            device_id_type=MESH,
        )

    def reduce_middle(turn):
        for relation, peer in enumerate(chan_peers):
            reduce_chan_copy(turn, relation, chan, peer).wait_send()
            reduce_chan_copy(turn, relation, peer, peer).wait_recv()
        total = red_chan[turn, 0] + red_chan[turn, 1] + red_chan[turn, 2] + red_chan[turn, 3]
        red_samp[turn, samp] = total

        def send(hop, carry):
            reduce_samp_copy(turn, hop, samp).start()
            return carry

        lax.fori_loop(1, samp_count, send, 0)

    def reduce_end(turn):
        def wait(hop, carry):
            reduce_samp_copy(turn, hop, samp).wait_send()
            reduce_samp_copy(turn, hop, (samp + hop) % samp_count).wait_recv()
            return carry

        lax.fori_loop(1, samp_count, wait, 0)

        def add(index, total):
            return total + red_samp[turn, index]

        total = lax.fori_loop(0, samp_count, add, jnp.zeros((24, LANES), F32))
        return [whole_sum(total[number * 8 : (number + 1) * 8]) for number in range(3)]

    gather_finish(0)
    exchange(0)

    def first_apply(block, carry):
        norm, dot, square = carry
        operand = sorted_loads[:, lane_tile(block)]
        mapped = apply_block(0, block, operand)
        image[:, lane_tile(block)] = mapped
        return norm + operand * operand, dot + operand * mapped, square + mapped * mapped

    sums = lax.fori_loop(0, blocks, first_apply, (nothing, nothing, nothing))
    reduce_begin(0, sums)
    reduce_middle(0)
    norm_now, dot, square = reduce_end(0)
    first_step = norm_now / dot
    norm_next = jnp.maximum(
        norm_now - 2.0 * first_step * dot + first_step * first_step * square, 0.0
    )
    ratio = norm_next / norm_now

    norm_sum = nothing
    for part in range(CHUNKS):
        for tile in range(part * per_chunk, (part + 1) * per_chunk):
            columns = slice(tile * LANES, (tile + 1) * LANES)
            operand = sorted_loads[:, columns]
            remainder = operand - first_step * image[:, columns]
            norm_sum = norm_sum + remainder * remainder
            step = remainder + ratio * operand
            direction[:, columns] = step
            gathered[1, chan, :, columns] = step.astype(BF16)
        gather_start(1, part)

    inv_sum[...] = jnp.zeros_like(inv_sum)
    lane_id = lax.broadcasted_iota(jnp.int32, (LANES, LANES), 1).astype(F32)
    sub_id = lax.broadcasted_iota(jnp.int32, (LANES, LANES), 0).astype(F32)

    def inverse_step(tile, carry):
        index = jnp.broadcast_to(perm[pl.ds(tile, 1), :].astype(F32), (LANES, LANES))
        target = index.T - lane_id
        position = sub_id + (tile * LANES).astype(F32)
        for part in range(blocks):
            hit = jnp.where(target == float(part * LANES), position, 0.0)
            inv_sum[part * 8 : (part + 1) * 8, :] += fold(hit)
        return carry

    lax.fori_loop(0, blocks, inverse_step, 0)
    for part in range(blocks):
        inverse[part : part + 1, :] = jnp.sum(
            inv_sum[part * 8 : (part + 1) * 8, :], axis=0, keepdims=True
        )
    for part in range(CHUNKS // 2):
        gather_forward(1, part)
    for part in range(CHUNKS // 2, CHUNKS):
        gather_forward(1, part)

    gather_finish(1)
    exchange(1)

    def second_apply(block, total):
        operand = direction[:, lane_tile(block)]
        mapped = apply_block(1, block, operand)
        res[:, lane_tile(block)] = mapped
        return total + operand * mapped

    dot_sum = lax.fori_loop(0, blocks, second_apply, nothing)
    reduce_begin(1, [norm_sum, dot_sum])
    reduce_middle(1)
    norm_last, dot_last, _ = reduce_end(1)
    second_step = norm_last / dot_last

    def output_step(tile, carry):
        columns = lane_tile(tile)
        right = sorted_loads[:, columns]
        sol[:, columns] = first_step * right + second_step * direction[:, columns]
        res[:, columns] = right - first_step * image[:, columns] - second_step * res[:, columns]
        return carry

    lax.fori_loop(0, blocks, output_step, 0)


def per_device(loads, coords, coreg_factor, noise, run_perm, block_nbrs, nbr_count):
    rows, runs = loads.shape
    blocks, slots = block_nbrs.shape
    samp_count = lax.axis_size("samp")
    halo = (slots - 1) * LANES
    extent = runs + 2 * halo
    chans = lax.axis_size("chan")
    vmem = pl.BlockSpec(memory_space=pltpu.VMEM)
    smem = pl.BlockSpec(memory_space=pltpu.SMEM)
    wide = pltpu.VMEM((rows, runs), F32)
    wide_out = jax.ShapeDtypeStruct((rows, runs), F32)
    index_rows = pltpu.VMEM((blocks, LANES), jnp.int32)
    limits = pltpu.CompilerParams(vmem_limit_bytes=48 * 2**20)
    perm = run_perm.reshape(blocks, LANES)
    sorted_loads, sorted_coords = pl.pallas_call(
        functools.partial(sorter, blocks),
        out_shape=[wide_out, jax.ShapeDtypeStruct((8, runs), F32)],
        in_specs=[vmem] * 3,
        out_specs=[vmem] * 2,
        scratch_shapes=[index_rows, pltpu.VMEM((8, runs), F32)],
        compiler_params=limits,
    )(loads, coords, perm)
    sorted_sol, sorted_res, inverse = pl.pallas_call(
        functools.partial(solver, samp_count, blocks, slots),
        out_shape=[wide_out, wide_out, jax.ShapeDtypeStruct((blocks, LANES), F32)],
        in_specs=[vmem] * 6 + [smem],
        out_specs=[vmem] * 3,
        scratch_shapes=[
            pltpu.VMEM((blocks * 8, LANES), F32),
            pltpu.VMEM((8, extent), F32),
            pltpu.VMEM((LANES, runs), BF16),
            pltpu.VMEM((extent // LANES, LANES, LANES), BF16),
            pltpu.VMEM((blocks, slots * LANES, LANES), BF16),
            pltpu.VMEM((chans, rows, coreg_factor.shape[1]), F32),
            pltpu.VMEM((3 * rows, chans * rows), BF16),
            wide, wide,
            pltpu.VMEM((2, chans, rows, runs), BF16),
            pltpu.VMEM((extent // LANES, rows, LANES), BF16),
            pltpu.VMEM((extent // LANES, rows, LANES), BF16),
            pltpu.VMEM((2, chans, 24, LANES), F32),
            pltpu.VMEM((2, samp_count, 24, LANES), F32),
            pltpu.SemaphoreType.DMA((3,)),
            pltpu.SemaphoreType.DMA((3,)),
            pltpu.SemaphoreType.DMA((2, 3, CHUNKS)),
            pltpu.SemaphoreType.DMA((2, 3, CHUNKS)),
            pltpu.SemaphoreType.DMA((3, 2)),
            pltpu.SemaphoreType.DMA((3, 2)),
            pltpu.SemaphoreType.DMA((2, 3)),
            pltpu.SemaphoreType.DMA((2, 3)),
            pltpu.SemaphoreType.DMA((2, samp_count)),
            pltpu.SemaphoreType.DMA((2, samp_count)),
        ],
        compiler_params=pltpu.CompilerParams(
            collective_id=0, has_side_effects=True, vmem_limit_bytes=56 * 2**20
        ),
    )(
        sorted_loads,
        sorted_coords,
        coreg_factor,
        noise[:, None],
        perm - lax.axis_index("samp") * runs,
        jnp.broadcast_to(nbr_count[:, None], (blocks, LANES)),
        block_nbrs[:, 0] - lax.axis_index("samp") * blocks + slots - 1,
    )
    return pl.pallas_call(
        functools.partial(unsorter, blocks),
        out_shape=[wide_out, wide_out],
        in_specs=[vmem] * 3,
        out_specs=[vmem] * 2,
        scratch_shapes=[index_rows],
        compiler_params=limits,
    )(sorted_sol, sorted_res, inverse)


def solution(mesh):
    return jax.shard_map(
        per_device,
        mesh=mesh,
        in_specs=(
            P("chan", "samp"),
            P(None, "samp"),
            P("chan", None),
            P("chan"),
            P("samp"),
            P("samp", None),
            P("samp"),
        ),
        out_specs=(P("chan", "samp"), P("chan", "samp")),
        check_vma=False,
    )
```

time: 563 us -> 119 us (0.21)
  blocking collectives: 131 us -> 0 us
  other arithmetic: 127 us -> 1.88 us
  Pallas kernels: 0 us -> 108 us
  local copies, waits for them, and re-layouts: 108 us -> 7.93 us
  waiting for transfers between devices: 67.2 us -> 0 us
  matrix products: 52.5 us -> 0 us
  loops' own time: 40.1 us -> 0 us
  between operations: 18.3 us -> 0.68 us
  starting transfers between devices: 14.9 us -> 0 us
    psum x3 -> x0, blocking collectives: 124 us -> none  [the longest x2 82.3 us: squared_norm(): return lax.psum(jnp.sum(remainder * remainder), ('samp', 'chan'))]
    pallas_call x0 -> x3, Pallas kernels: none -> 108 us  [the longest x1 84 us: per_device(): pl.pallas_call(functools.partial(solver, samp_count, blocks, slots), out_...]
    gather x40 -> x0, local copies, waits for them, and re-layouts: 70.9 us -> none  [the longest x24 45.4 us: slot_step(): partner_vals = jnp.take(value_blocks, partner_ids, axis=1)]
    dynamic_update_slice x12 -> x0, other arithmetic: 56.4 us -> none  [per_device(): all_tiles = lax.map(build_tile, jnp.arange(slot_limit, dtype=jnp.int32))]
    dot_general x27 -> x0, matrix products: 52.5 us -> none  [the longest x24 44.9 us: slot_step(): jnp.einsum('bim,cbm->cbi', kernel_tile, partner_vals, preferred_element_t...]
    reduce_scatter x2 -> x0, waiting for transfers between devices: 51 us -> none  [per_device(): lax.psum_scatter(jnp.dot(coreg_cols, rounded_wide, precision=lax.Precisio...]
    another operation x3 -> x0, loops' own time: 40.1 us -> none  [the longest x1 23.4 us: per_device(): all_tiles = lax.map(build_tile, jnp.arange(slot_limit, dtype=jnp.int32))]
    and x25 -> x0, other arithmetic: 17.4 us -> none  [the longest x24 16.7 us: slot_step(): partner_vals = jnp.take(value_blocks, partner_ids, axis=1)]
  transfers between devices with their start and end apart: 8 -> 0, of which waited for: 4 -> 0; matrix products, arithmetic and copies ran while one was open for 19% -> 0% of each run, Pallas kernels for 0% -> 0%
where the time goes in v1:
time: 119 us; the launch traced here: 118 us
  Pallas kernels  108 us (91%)
  local copies, waits for them, and re-layouts  7.93 us (7%)
  other arithmetic  1.88 us (2%)
    pallas_call x1, Pallas kernels, per_device(): pl.pallas_call(functools.partial(solver, samp_count, blocks, slots), out_...  84 us
    pallas_call x1, Pallas kernels, per_device(): pl.pallas_call(functools.partial(unsorter, blocks), out_shape=[wide_out,...  14.5 us
    pallas_call x1, Pallas kernels, per_device(): pl.pallas_call(functools.partial(sorter, blocks), out_shape=[wide_out, ja...  9.35 us
    unnamed x20, local copies, waits for them, and re-layouts  6.57 us

profile of v1, /device:TPU:0, one launch (start us, length us, event | category | flops | bytes accessed | tf_op | source)
XLA Modules:
  0.0 118.3 jit_solution(5243385653367943219)
XLA Ops:
  0.6 0.0 copy-start.6
  0.6 1.3 %add_bitcast_fusion.first_block = s32[24]{0:T(128)} fusion(s32[24,12]{0,1:T(8,128)} %param.12, s32[]{:T(128)S(6)} %mul.7), kind=kLoop, calls=%fused_computation.1 | loop fusion | flops 48 | bytes 196 | tf_op jit(solution)/shard_map/sub | solution.py:521
  1.9 0.0 copy-done.6
  1.9 0.0 copy-start.9
  1.9 0.6 broadcast_subtract_fusion.perm
  2.5 0.1 copy-done.9
  2.6 0.0 copy-start.8
  2.6 0.7 broadcast_in_dim.10.counts
  3.3 0.0 copy-done.8
  3.3 0.7 copy.9.noise
  4.0 0.0 copy-start
  4.0 1.1 copy-done
  5.1 0.0 copy-start.4
  5.1 0.9 copy-done.4
  6.0 9.4 %shard_map.86 = (f32[64,3072]{1,0:T(8,128)S(1)}, f32[8,3072]{1,0:T(8,128)S(1)}) custom-call(f32[64,3072]{1,0:T(8,128)S(1)} %copy-done, f32[6,3072]{1,0:T(8,128)S(1)} %copy-done.4, s32[24,128]{1,0:T(8,128)S(1)} %bitcast.5), custom_call_target="tpu_custom_call" | custom-call | tf_op jit(solution)/shard_map/pallas_call | solution.py:473
  15.3 0.0 copy-start.3
  15.4 0.9 copy-done.3
  16.2 0.6 copy-done.5
  16.9 84.0 %shard_map.87 = (f32[64,3072]{1,0:T(8,128)}, f32[64,3072]{1,0:T(8,128)}, f32[24,128]{1,0:T(8,128)}) custom-call(f32[64,3072]{1,0:T(8,128)} %copy-done.3, f32[8,3072]{1,0:T(8,128)} %copy-done.5, f32[64,256]{1,0:T(8,128)} %factor.1, f32[64,1]{1,0:T(8,128)} %copy.9.noise, s32[24,128]{1,0:T(8,128)} %broadcast_subtract_fusion.perm, ...), custom_call_target="tpu_custom_call" | custom-call | tf_op jit(solution)/shard_map/pallas_call | solution.py:481
  100.9 0.0 copy-start.1
  100.9 1.1 copy-done.1
  102.0 1.1 copy-done.2
  103.1 0.7 copy-done.7
  103.8 14.5 %shard_map.88 = (f32[64,3072]{1,0:T(8,128)}, f32[64,3072]{1,0:T(8,128)}) custom-call(f32[64,3072]{1,0:T(8,128)S(1)} %copy-done.1, f32[64,3072]{1,0:T(8,128)S(1)} %copy-done.2, f32[24,128]{1,0:T(8,128)S(1)} %copy-done.7), custom_call_target="tpu_custom_call" | custom-call | tf_op jit(solution)/shard_map/pallas_call | solution.py:523
  (3 shorter events, 0.0 us)
Async XLA Ops:
  0.6 1.3 %copy-start.6 = (s32[3072]{0:T(1024)S(1)}, s32[3072]{0:T(1024)}, u32[]{:S(2)}) copy-start(s32[3072]{0:T(1024)} %param.11) | copy-start | bytes 36868
  1.9 0.7 copy-start.9
  2.6 0.7 copy-start.8
  4.0 1.1 copy-start
  5.1 0.9 copy-start.4
  15.3 0.9 copy-start.3
  16.2 0.6 copy-start.5
  100.9 1.1 copy-start.1
  102.0 1.1 copy-start.2
  103.1 0.7 copy-start.7

commit v2 on v1

--- a/solution.py
+++ b/solution.py
@@ -20,25 +20,6 @@
     return pl.ds(pl.multiple_of(index * LANES, LANES), LANES)
 
 
-def permute_tiles(source, order, target, begin, end):
-    rows, columns = source.shape
-
-    def step(tile, carry):
-        index = order[pl.ds(tile, 1), :]
-        lane = jnp.broadcast_to(index % LANES, (rows, LANES))
-        origin = jnp.broadcast_to(index // LANES, (rows, LANES))
-        result = jnp.zeros((rows, LANES), F32)
-        for part in range(columns // LANES):
-            picked = jnp.take_along_axis(
-                source[:, part * LANES : (part + 1) * LANES], lane, axis=1, mode="promise_in_bounds"
-            )
-            result = jnp.where(origin == part, picked, result)
-        target[:, lane_tile(tile)] = result
-        return carry
-
-    lax.fori_loop(begin, end, step, 0)
-
-
 def pieces(value):
     high = value.astype(BF16).astype(F32)
     rest = value - high
@@ -57,31 +38,17 @@
     return jnp.sum(jnp.sum(value, axis=0, keepdims=True), axis=1, keepdims=True)
 
 
-def sorter(blocks, loads, coords, perm, sorted_loads, sorted_coords, order, coords_in):
-    order[...] = perm[...] - lax.axis_index("samp") * loads.shape[1]
-    coords_in[...] = jnp.zeros_like(coords_in)
-    coords_in[0 : coords.shape[0], :] = coords[...] * (1.0 / SUPPORT)
-    permute_tiles(coords_in, order, sorted_coords, 0, blocks)
-    permute_tiles(loads, order, sorted_loads, 0, blocks)
-
-
-def unsorter(blocks, sorted_sol, sorted_res, inverse, sol, res, order):
-    order[...] = inverse[...].astype(jnp.int32)
-    permute_tiles(sorted_sol, order, sol, 0, blocks)
-    permute_tiles(sorted_res, order, res, 0, blocks)
-
-
 def solver(
     samp_count, blocks, slots,
-    sorted_loads, sorted_coords, factor, noise, perm, counts, first_block,
-    sol, res, inverse,
-    inv_sum, coords_ext, own_terms, ext_terms, tiles,
+    loads, coords, factor, noise, perm, nbrs, counts,
+    sol, res,
+    source, spread, sorted_loads, position, perm_rows, perm_column, image_out, coords_ext, own_terms, ext_terms, tiles,
     factors, coreg, direction, image, gathered, values_first, values_second,
     red_chan, red_samp,
     fac_send, fac_recv, gat_send, gat_recv, halo_send, halo_recv,
     rc_send, rc_recv, rs_send, rs_recv,
 ):
-    rows, runs = sorted_loads.shape
+    rows, runs = loads.shape
     halo = (slots - 1) * LANES
     extent = runs + 2 * halo
     edge = slots - 1
@@ -106,7 +73,80 @@
 
     lax.fori_loop(1, samp_count, greet, 0)
 
-    coords_ext[:, halo : halo + runs] = sorted_coords[...]
+    perm_rows[...] = perm[...] - samp * runs
+    stride = 2 * LANES
+    for begin in range(0, runs, stride):
+        columns = slice(begin, begin + stride)
+        parts = pieces(
+            jnp.concatenate(
+                [
+                    loads[:, columns],
+                    coords[:, columns] * (1.0 / SUPPORT),
+                    jnp.zeros((8 - coords.shape[0], stride), F32),
+                ],
+                axis=0,
+            )
+        )
+        source[:, columns] = jnp.concatenate(parts, axis=0).astype(BF16)
+    depth = runs // 6
+    for begin in range(0, depth, LANES):
+        position[begin : begin + LANES, :] = (
+            lax.broadcasted_iota(jnp.int32, (LANES, stride), 0) + begin
+        )
+
+    def sort_step(pair, carry):
+        columns = pl.ds(pl.multiple_of(pair * stride, stride), stride)
+        target = perm_rows[:, columns]
+        total = jnp.zeros((3 * (rows + 8), stride), F32)
+        for part in range(6):
+            chosen = jnp.where(position[...] == target - part * depth, 1.0, 0.0).astype(BF16)
+            total = total + jnp.dot(
+                source[:, part * depth : (part + 1) * depth],
+                chosen,
+                preferred_element_type=F32,
+            )
+        high, middle, low = (total[n * (rows + 8) : (n + 1) * (rows + 8)] for n in range(3))
+        result = high + middle + low
+        sorted_loads[:, columns] = result[0:rows]
+        coords_ext[:, pl.ds(pl.multiple_of(halo + pair * stride, LANES), stride)] = result[rows:]
+        return carry
+
+    def column_step(tile, carry):
+        index = perm_rows[:, lane_tile(tile)].astype(F32)
+        perm_column[lane_tile(tile), :] = jnp.broadcast_to(index, (LANES, LANES)).T
+        return carry
+
+    lane_id = lax.broadcasted_iota(jnp.int32, (1, LANES), 1).astype(F32)
+
+    def unsort(block_sums, target):
+        for begin in range(0, runs, stride):
+            columns = slice(begin, begin + stride)
+            high, middle, _ = pieces(block_sums[:, columns])
+            spread[:, columns] = jnp.concatenate([high, middle], axis=0).astype(BF16)
+
+        def unsort_step(pair, carry):
+            columns = pl.ds(pl.multiple_of(pair * stride, stride), stride)
+            low_lanes = lane_id + (pair * stride).astype(F32)
+            total = jnp.zeros((2 * rows, stride), F32)
+            for part in range(6):
+                index = perm_column[part * depth : (part + 1) * depth, :]
+                chosen = jnp.concatenate(
+                    [
+                        jnp.where(index == low_lanes, 1.0, 0.0).astype(BF16),
+                        jnp.where(index == low_lanes + float(LANES), 1.0, 0.0).astype(BF16),
+                    ],
+                    axis=1,
+                )
+                total = total + jnp.dot(
+                    spread[:, part * depth : (part + 1) * depth],
+                    chosen,
+                    preferred_element_type=F32,
+                )
+            target[:, columns] = total[0:rows] + total[rows:]
+            return carry
+
+        lax.fori_loop(0, runs // stride, unsort_step, 0)
+
 
     @pl.when(samp == 0)
     def _():
@@ -163,12 +203,6 @@
         def _():
             copies[1].wait_send()
             copies[0].wait_recv()
-
-    coord_copies = halo_copies(
-        [coords_ext.at[:, pl.ds(first, halo)] for first in (halo, runs, 0, extent - halo)], 0
-    )
-    halo_start_low(coord_copies)
-    halo_start_high(coord_copies)
 
     factor_copies = []
     for relation, peer in enumerate(chan_peers):
@@ -212,15 +246,23 @@
             gather_copy(turn, 2, part, 3 - chan, core_peer).wait_recv()
 
     per_chunk = blocks // CHUNKS
+    pairs = runs // stride // CHUNKS
     for part in range(CHUNKS):
+        lax.fori_loop(part * pairs, (part + 1) * pairs, sort_step, 0)
         columns = pl.ds(part * chunk, chunk)
         gathered[0, chan, :, columns] = sorted_loads[:, columns].astype(BF16)
         gather_start(0, part)
 
+    coord_copies = halo_copies(
+        [coords_ext.at[:, pl.ds(first, halo)] for first in (halo, runs, 0, extent - halo)], 0
+    )
+    halo_start_low(coord_copies)
+    halo_start_high(coord_copies)
+
     row_id = lax.broadcasted_iota(jnp.int32, (8, LANES), 0)
 
     def own_step(tile, carry):
-        point = sorted_coords[:, lane_tile(tile)]
+        point = coords_ext[:, lane_tile(tile + edge)]
         norm = jnp.sum(point * point, axis=0, keepdims=True)
         terms = jnp.where(row_id == 6, 1.0, jnp.where(row_id == 7, norm, -2.0 * point))
         high, middle, low = pieces(terms)
@@ -247,11 +289,11 @@
     lax.fori_loop(0, extent // LANES, ext_step, 0)
 
     def window_start(block):
-        return first_block[block]
+        return jnp.clip(nbrs[block, 0] - samp * blocks + edge, 0, widened - slots)
 
     def tile_step(block, carry):
         start = window_start(block)
-        count = counts[pl.ds(block, 1), :]
+        count = jnp.full((1, LANES), counts[block], jnp.int32)
         own = own_terms[:, lane_tile(block)]
         for slot in range(slots):
             partner = ext_terms[start + slot]
@@ -312,7 +354,11 @@
             mix(turn, halo, runs - halo)
         halo_wait(copies)
 
-    noise_wide = jnp.broadcast_to(noise[...], (rows, LANES))
+    diagonal = lax.broadcasted_iota(jnp.int32, (rows, rows), 0) == lax.broadcasted_iota(
+        jnp.int32, (rows, rows), 1
+    )
+    noise_column = jnp.sum(jnp.where(diagonal, noise[...], 0.0), axis=1, keepdims=True)
+    noise_wide = jnp.broadcast_to(noise_column, (rows, LANES))
     nothing = jnp.zeros((rows, LANES), F32)
 
     def apply_block(turn, block, operand):
@@ -408,26 +454,10 @@
             gathered[1, chan, :, columns] = step.astype(BF16)
         gather_start(1, part)
 
-    inv_sum[...] = jnp.zeros_like(inv_sum)
-    lane_id = lax.broadcasted_iota(jnp.int32, (LANES, LANES), 1).astype(F32)
-    sub_id = lax.broadcasted_iota(jnp.int32, (LANES, LANES), 0).astype(F32)
-
-    def inverse_step(tile, carry):
-        index = jnp.broadcast_to(perm[pl.ds(tile, 1), :].astype(F32), (LANES, LANES))
-        target = index.T - lane_id
-        position = sub_id + (tile * LANES).astype(F32)
-        for part in range(blocks):
-            hit = jnp.where(target == float(part * LANES), position, 0.0)
-            inv_sum[part * 8 : (part + 1) * 8, :] += fold(hit)
-        return carry
-
-    lax.fori_loop(0, blocks, inverse_step, 0)
-    for part in range(blocks):
-        inverse[part : part + 1, :] = jnp.sum(
-            inv_sum[part * 8 : (part + 1) * 8, :], axis=0, keepdims=True
-        )
+    lax.fori_loop(0, blocks, column_step, 0)
     for part in range(CHUNKS // 2):
         gather_forward(1, part)
+    unsort(image, image_out)
     for part in range(CHUNKS // 2, CHUNKS):
         gather_forward(1, part)
 
@@ -437,20 +467,23 @@
     def second_apply(block, total):
         operand = direction[:, lane_tile(block)]
         mapped = apply_block(1, block, operand)
-        res[:, lane_tile(block)] = mapped
+        image[:, lane_tile(block)] = mapped
         return total + operand * mapped
 
     dot_sum = lax.fori_loop(0, blocks, second_apply, nothing)
     reduce_begin(1, [norm_sum, dot_sum])
     reduce_middle(1)
+    unsort(image, direction)
     norm_last, dot_last, _ = reduce_end(1)
     second_step = norm_last / dot_last
 
     def output_step(tile, carry):
         columns = lane_tile(tile)
-        right = sorted_loads[:, columns]
-        sol[:, columns] = first_step * right + second_step * direction[:, columns]
-        res[:, columns] = right - first_step * image[:, columns] - second_step * res[:, columns]
+        right = loads[:, columns]
+        remainder = right - first_step * image_out[:, columns]
+        step = remainder + ratio * right
+        sol[:, columns] = first_step * right + second_step * step
+        res[:, columns] = remainder - second_step * direction[:, columns]
         return carry
 
     lax.fori_loop(0, blocks, output_step, 0)
@@ -467,24 +500,19 @@
     smem = pl.BlockSpec(memory_space=pltpu.SMEM)
     wide = pltpu.VMEM((rows, runs), F32)
     wide_out = jax.ShapeDtypeStruct((rows, runs), F32)
-    index_rows = pltpu.VMEM((blocks, LANES), jnp.int32)
-    limits = pltpu.CompilerParams(vmem_limit_bytes=48 * 2**20)
-    perm = run_perm.reshape(blocks, LANES)
-    sorted_loads, sorted_coords = pl.pallas_call(
-        functools.partial(sorter, blocks),
-        out_shape=[wide_out, jax.ShapeDtypeStruct((8, runs), F32)],
-        in_specs=[vmem] * 3,
+    return pl.pallas_call(
+        functools.partial(solver, samp_count, blocks, slots),
+        out_shape=[wide_out, wide_out],
+        in_specs=[vmem] * 5 + [smem] * 2,
         out_specs=[vmem] * 2,
-        scratch_shapes=[index_rows, pltpu.VMEM((8, runs), F32)],
-        compiler_params=limits,
-    )(loads, coords, perm)
-    sorted_sol, sorted_res, inverse = pl.pallas_call(
-        functools.partial(solver, samp_count, blocks, slots),
-        out_shape=[wide_out, wide_out, jax.ShapeDtypeStruct((blocks, LANES), F32)],
-        in_specs=[vmem] * 6 + [smem],
-        out_specs=[vmem] * 3,
         scratch_shapes=[
-            pltpu.VMEM((blocks * 8, LANES), F32),
+            pltpu.VMEM((3 * (rows + 8), runs), BF16),
+            pltpu.VMEM((2 * rows, runs), BF16),
+            wide,
+            pltpu.VMEM((runs // 6, 2 * LANES), jnp.int32),
+            pltpu.VMEM((1, runs), jnp.int32),
+            pltpu.VMEM((runs, LANES), F32),
+            wide,
             pltpu.VMEM((8, extent), F32),
             pltpu.VMEM((LANES, runs), BF16),
             pltpu.VMEM((extent // LANES, LANES, LANES), BF16),
@@ -512,22 +540,14 @@
             collective_id=0, has_side_effects=True, vmem_limit_bytes=56 * 2**20
         ),
     )(
-        sorted_loads,
-        sorted_coords,
+        loads,
+        coords,
         coreg_factor,
-        noise[:, None],
-        perm - lax.axis_index("samp") * runs,
-        jnp.broadcast_to(nbr_count[:, None], (blocks, LANES)),
-        block_nbrs[:, 0] - lax.axis_index("samp") * blocks + slots - 1,
+        noise[None, :],
+        run_perm[None, :],
+        block_nbrs,
+        nbr_count,
     )
-    return pl.pallas_call(
-        functools.partial(unsorter, blocks),
-        out_shape=[wide_out, wide_out],
-        in_specs=[vmem] * 3,
-        out_specs=[vmem] * 2,
-        scratch_shapes=[index_rows],
-        compiler_params=limits,
-    )(sorted_sol, sorted_res, inverse)
 
 
 def solution(mesh):

time: 119 us -> 97.8 us (0.82)
  Pallas kernels: 108 us -> 92.6 us
  local copies, waits for them, and re-layouts: 7.93 us -> 4.4 us
  other arithmetic: 1.88 us -> 0 us
    pallas_call x2 -> x0, Pallas kernels: 23.8 us -> none  [the longest x1 14.5 us: per_device(): pl.pallas_call(functools.partial(unsorter, blocks), out_shape=[wide_out,...]
    pallas_call x1, Pallas kernels: 84 us -> 92.6 us  [per_device(): pl.pallas_call(functools.partial(solver, samp_count, blocks, slots), out_...]
    unnamed x20 -> x5, local copies, waits for them, and re-layouts: 6.57 us -> 4.4 us
    sub x2 -> x0, other arithmetic: 1.88 us -> none  [the longest x1 1.28 us: per_device(): block_nbrs[:, 0] - lax.axis_index('samp') * blocks + slots - 1]
    broadcast_in_dim x2 -> x0, local copies, waits for them, and re-layouts: 1.36 us -> none  [the longest x1 0.7 us: per_device(): noise[:, None]]
where the time goes in v2:
time: 97.8 us; the launch traced here: 97.6 us
  Pallas kernels  92.6 us (95%)
  local copies, waits for them, and re-layouts  4.4 us (4%)
    pallas_call x1, Pallas kernels, per_device(): pl.pallas_call(functools.partial(solver, samp_count, blocks, slots), out_...  92.6 us
    unnamed x5, local copies, waits for them, and re-layouts  4.4 us

profile of v2, /device:TPU:0, one launch (start us, length us, event | category | flops | bytes accessed | tf_op | source)
XLA Modules:
  0.0 97.6 jit_solution(651105108561990965)
XLA Ops:
  0.6 1.4 %copy.9.nbrs = s32[24,12]{1,0:T(8,128)} copy(s32[24,12]{0,1:T(8,128)} %param.12) | data formatting | bytes 2304 | tf_op args[5]
  2.0 92.6 %shard_map.86 = (f32[64,3072]{1,0:T(8,128)}, f32[64,3072]{1,0:T(8,128)}) custom-call(f32[64,3072]{1,0:T(8,128)} %loads.1, f32[6,3072]{1,0:T(8,128)} %coords.1, f32[64,256]{1,0:T(8,128)} %factor.1, f32[1,64]{1,0:T(1,128)} %bitcast.3, s32[1,3072]{1,0:T(1,128)} %bitcast.2, s32[24,12]{1,0:T(8,128)} %copy.9.nbrs, s32[24]{0:T(128)} %counts.1), custom_call_target="tpu_custom_call" | custom-call | tf_op jit(solution)/shard_map/pallas_call | solution.py:503
  94.6 0.0 copy-start
  94.6 2.1 %copy.12 = f32[64,3072]{1,0:T(8,128)} copy(f32[64,3072]{1,0:T(8,128)} %get-tuple-element.4) | data formatting | bytes 1572864
  96.7 0.0 copy-done
  96.7 0.9 copy.13
Async XLA Ops:
  94.6 2.2 %copy-start = (f32[64,3072]{1,0:T(8,128)S(1)}, f32[64,3072]{1,0:T(8,128)}, u32[]{:S(2)}) copy-start(f32[64,3072]{1,0:T(8,128)} %get-tuple-element.5) | copy-start | bytes 2359300

commit v3 on v2

--- a/solution.py
+++ b/solution.py
@@ -41,8 +41,8 @@
 def solver(
     samp_count, blocks, slots,
     loads, coords, factor, noise, perm, nbrs, counts,
-    sol, res,
-    source, spread, sorted_loads, position, perm_rows, perm_column, image_out, coords_ext, own_terms, ext_terms, tiles,
+    image_out, second_out, scalars,
+    source, spread, sorted_loads, position, perm_rows, perm_column, coords_ext, own_terms, ext_terms, tiles,
     factors, coreg, direction, image, gathered, values_first, values_second,
     red_chan, red_samp,
     fac_send, fac_recv, gat_send, gat_recv, halo_send, halo_recv,
@@ -118,12 +118,13 @@
 
     lane_id = lax.broadcasted_iota(jnp.int32, (1, LANES), 1).astype(F32)
 
-    def unsort(block_sums, target):
+    def unsort_begin(block_sums):
         for begin in range(0, runs, stride):
             columns = slice(begin, begin + stride)
             high, middle, _ = pieces(block_sums[:, columns])
             spread[:, columns] = jnp.concatenate([high, middle], axis=0).astype(BF16)
 
+    def unsort(target, begin, end):
         def unsort_step(pair, carry):
             columns = pl.ds(pl.multiple_of(pair * stride, stride), stride)
             low_lanes = lane_id + (pair * stride).astype(F32)
@@ -145,7 +146,7 @@
             target[:, columns] = total[0:rows] + total[rows:]
             return carry
 
-        lax.fori_loop(0, runs // stride, unsort_step, 0)
+        lax.fori_loop(begin, end, unsort_step, 0)
 
 
     @pl.when(samp == 0)
@@ -163,46 +164,66 @@
     factors[chan] = factor[...]
     pl.semaphore_wait(barrier, 3 + samp_count - 1)
 
-    def halo_copies(regions, turn):
-        own_low, own_high, low, high = regions
-        to_low = pltpu.make_async_remote_copy(
-            src_ref=own_low,
-            dst_ref=high,
-            send_sem=halo_send.at[turn, 0],
-            recv_sem=halo_recv.at[turn, 0],
-            device_id={"samp": (samp + samp_count - 1) % samp_count},
+    per_chunk = blocks // CHUNKS
+    below = (samp + samp_count - 1) % samp_count
+    above = (samp + 1) % samp_count
+
+    def halo_copy(source_ref, target_ref, turn, side, part):
+        return pltpu.make_async_remote_copy(
+            src_ref=source_ref,
+            dst_ref=target_ref,
+            send_sem=halo_send.at[turn, side, part],
+            recv_sem=halo_recv.at[turn, side, part],
+            device_id={"samp": below if side == 0 else above},
             device_id_type=MESH,
         )
-        to_high = pltpu.make_async_remote_copy(
-            src_ref=own_high,
-            dst_ref=low,
-            send_sem=halo_send.at[turn, 1],
-            recv_sem=halo_recv.at[turn, 1],
-            device_id={"samp": (samp + 1) % samp_count},
-            device_id_type=MESH,
-        )
-        return to_low, to_high
-
-    def halo_start_low(copies):
-        @pl.when(samp > 0)
-        def _():
-            copies[0].start()
-
-    def halo_start_high(copies):
-        @pl.when(samp < samp_count - 1)
-        def _():
-            copies[1].start()
+
+    def halo_start(copies):
+        for side, group in enumerate(copies):
+            if group:
+                @pl.when((samp > 0) if side == 0 else (samp < samp_count - 1))
+                def _():
+                    for copy in group:
+                        copy.start()
 
     def halo_wait(copies):
         @pl.when(samp > 0)
         def _():
-            copies[0].wait_send()
-            copies[1].wait_recv()
+            for copy in copies[0]:
+                copy.wait_send()
+            for copy in copies[1]:
+                copy.wait_recv()
 
         @pl.when(samp < samp_count - 1)
         def _():
-            copies[1].wait_send()
-            copies[0].wait_recv()
+            for copy in copies[1]:
+                copy.wait_send()
+            for copy in copies[0]:
+                copy.wait_recv()
+
+    def value_copies(turn, part):
+        buffer = values[turn]
+        begin, end = part * per_chunk, (part + 1) * per_chunk
+        result = ([], [])
+        if begin < edge:
+            count = min(end, edge) - begin
+            result[0].append(
+                halo_copy(
+                    buffer.at[pl.ds(edge + begin, count)],
+                    buffer.at[pl.ds(edge + blocks + begin, count)],
+                    turn + 1, 0, part,
+                )
+            )
+        if end > blocks - edge:
+            first = max(begin, blocks - edge)
+            result[1].append(
+                halo_copy(
+                    buffer.at[pl.ds(edge + first, end - first)],
+                    buffer.at[pl.ds(edge + first - blocks, end - first)],
+                    turn + 1, 1, part,
+                )
+            )
+        return result
 
     factor_copies = []
     for relation, peer in enumerate(chan_peers):
@@ -237,15 +258,13 @@
         gather_copy(turn, 1, part, far_peer, far_peer).wait_recv()
         gather_copy(turn, 2, part, far_peer, core_peer).start()
 
-    def gather_finish(turn):
-        for part in range(CHUNKS):
-            gather_copy(turn, 0, part, chan, core_peer).wait_send()
-            gather_copy(turn, 1, part, chan, far_peer).wait_send()
-            gather_copy(turn, 2, part, far_peer, core_peer).wait_send()
-            gather_copy(turn, 0, part, core_peer, core_peer).wait_recv()
-            gather_copy(turn, 2, part, 3 - chan, core_peer).wait_recv()
-
-    per_chunk = blocks // CHUNKS
+    def gather_finish(turn, part):
+        gather_copy(turn, 0, part, chan, core_peer).wait_send()
+        gather_copy(turn, 1, part, chan, far_peer).wait_send()
+        gather_copy(turn, 2, part, far_peer, core_peer).wait_send()
+        gather_copy(turn, 0, part, core_peer, core_peer).wait_recv()
+        gather_copy(turn, 2, part, 3 - chan, core_peer).wait_recv()
+
     pairs = runs // stride // CHUNKS
     for part in range(CHUNKS):
         lax.fori_loop(part * pairs, (part + 1) * pairs, sort_step, 0)
@@ -253,11 +272,17 @@
         gathered[0, chan, :, columns] = sorted_loads[:, columns].astype(BF16)
         gather_start(0, part)
 
-    coord_copies = halo_copies(
-        [coords_ext.at[:, pl.ds(first, halo)] for first in (halo, runs, 0, extent - halo)], 0
+    coord_copies = (
+        [halo_copy(
+            coords_ext.at[:, pl.ds(halo, halo)],
+            coords_ext.at[:, pl.ds(extent - halo, halo)],
+            0, 0, 0,
+        )],
+        [halo_copy(
+            coords_ext.at[:, pl.ds(runs, halo)], coords_ext.at[:, pl.ds(0, halo)], 0, 1, 0
+        )],
     )
-    halo_start_low(coord_copies)
-    halo_start_high(coord_copies)
+    halo_start(coord_copies)
 
     row_id = lax.broadcasted_iota(jnp.int32, (8, LANES), 0)
 
@@ -289,7 +314,7 @@
     lax.fori_loop(0, extent // LANES, ext_step, 0)
 
     def window_start(block):
-        return jnp.clip(nbrs[block, 0] - samp * blocks + edge, 0, widened - slots)
+        return jnp.clip(nbrs[0, block] - samp * blocks + edge, 0, widened - slots)
 
     def tile_step(block, carry):
         start = window_start(block)
@@ -307,12 +332,6 @@
             tiles[block, slot * LANES : (slot + 1) * LANES, :] = tile.astype(BF16)
         return carry
 
-    first_part = (blocks * 5) // 8
-    lax.fori_loop(0, first_part, tile_step, 0)
-    for part in range(CHUNKS):
-        gather_forward(0, part)
-    lax.fori_loop(first_part, blocks, tile_step, 0)
-
     for copy in factor_copies:
         copy.wait()
     coreg_rows = lax.dot_general(
@@ -325,34 +344,22 @@
     for number, piece in enumerate(pieces(coreg_rows)):
         coreg[number * rows : (number + 1) * rows, :] = piece.astype(BF16)
 
-    def mix(turn, begin, end):
-        weights = coreg[...]
-        while begin < end:
-            width = min(2 * LANES, end - begin)
-            operand = gathered[turn, :, :, begin : begin + width].reshape(4 * rows, width)
-            product = jnp.dot(weights, operand, preferred_element_type=F32)
+    def mix(turn, part):
+        gather_finish(turn, part)
+        for begin in range(part * chunk, (part + 1) * chunk, stride):
+            operand = gathered[turn, :, :, begin : begin + stride].reshape(4 * rows, stride)
+            product = jnp.dot(coreg[...], operand, preferred_element_type=F32)
             mixed = product[0:rows] + product[rows : 2 * rows] + product[2 * rows : 3 * rows]
-            for part in range(width // LANES):
-                values[turn][edge + begin // LANES + part] = mixed[
-                    :, part * LANES : (part + 1) * LANES
+            for half in range(2):
+                values[turn][edge + begin // LANES + half] = mixed[
+                    :, half * LANES : (half + 1) * LANES
                 ].astype(BF16)
-            begin += width
-
-    def exchange(turn):
-        copies = halo_copies(
-            [
-                values[turn].at[pl.ds(first, edge)]
-                for first in (edge, blocks, 0, widened - edge)
-            ],
-            turn + 1,
-        )
-        mix(turn, 0, halo)
-        halo_start_low(copies)
-        if runs - halo >= halo:
-            mix(turn, runs - halo, runs)
-            halo_start_high(copies)
-            mix(turn, halo, runs - halo)
-        halo_wait(copies)
+        copies = value_copies(turn, part)
+        halo_start(copies)
+        return copies
+
+    def merge(groups):
+        return tuple([copy for group in groups for copy in group[side]] for side in range(2))
 
     diagonal = lax.broadcasted_iota(jnp.int32, (rows, rows), 0) == lax.broadcasted_iota(
         jnp.int32, (rows, rows), 1
@@ -378,10 +385,11 @@
         )
 
     def reduce_begin(turn, parts):
-        for number, part in enumerate(parts):
-            red_chan[turn, chan, number * 8 : (number + 1) * 8, :] = fold(part)
-        for number in range(len(parts), 3):
-            red_chan[turn, chan, number * 8 : (number + 1) * 8, :] = jnp.zeros((8, LANES), F32)
+        lines = []
+        for part in parts:
+            lines.append(jnp.sum(fold(part), axis=0, keepdims=True))
+        lines.append(jnp.zeros((8 - len(parts), LANES), F32))
+        red_chan[turn, chan] = jnp.concatenate(lines, axis=0)
         for relation, peer in enumerate(chan_peers):
             reduce_chan_copy(turn, relation, chan, peer).start()
 
@@ -419,11 +427,20 @@
         def add(index, total):
             return total + red_samp[turn, index]
 
-        total = lax.fori_loop(0, samp_count, add, jnp.zeros((24, LANES), F32))
-        return [whole_sum(total[number * 8 : (number + 1) * 8]) for number in range(3)]
-
-    gather_finish(0)
-    exchange(0)
+        total = lax.fori_loop(0, samp_count, add, jnp.zeros((8, LANES), F32))
+        return [whole_sum(total[number : number + 1]) for number in range(3)]
+
+    eighth = blocks // 8
+    lax.fori_loop(0, eighth, tile_step, 0)
+    gather_forward(0, 0)
+    gather_forward(0, 1)
+    lax.fori_loop(eighth, 2 * eighth, tile_step, 0)
+    gather_forward(0, 2)
+    gather_forward(0, 3)
+    lax.fori_loop(2 * eighth, 3 * eighth, tile_step, 0)
+    copies = [mix(0, 0), mix(0, 1), mix(0, 2), mix(0, 3)]
+    lax.fori_loop(3 * eighth, blocks, tile_step, 0)
+    halo_wait(merge(copies))
 
     def first_apply(block, carry):
         norm, dot, square = carry
@@ -455,14 +472,15 @@
         gather_start(1, part)
 
     lax.fori_loop(0, blocks, column_step, 0)
-    for part in range(CHUNKS // 2):
+    unsort_begin(image)
+    copies = []
+    for part in range(CHUNKS):
+        unsort(image_out, part * pairs, (part + 1) * pairs)
         gather_forward(1, part)
-    unsort(image, image_out)
-    for part in range(CHUNKS // 2, CHUNKS):
-        gather_forward(1, part)
-
-    gather_finish(1)
-    exchange(1)
+        if part:
+            copies.append(mix(1, part - 1))
+    copies.append(mix(1, CHUNKS - 1))
+    halo_wait(merge(copies))
 
     def second_apply(block, total):
         operand = direction[:, lane_tile(block)]
@@ -473,20 +491,13 @@
     dot_sum = lax.fori_loop(0, blocks, second_apply, nothing)
     reduce_begin(1, [norm_sum, dot_sum])
     reduce_middle(1)
-    unsort(image, direction)
+    unsort_begin(image)
+    unsort(second_out, 0, runs // stride)
     norm_last, dot_last, _ = reduce_end(1)
     second_step = norm_last / dot_last
-
-    def output_step(tile, carry):
-        columns = lane_tile(tile)
-        right = loads[:, columns]
-        remainder = right - first_step * image_out[:, columns]
-        step = remainder + ratio * right
-        sol[:, columns] = first_step * right + second_step * step
-        res[:, columns] = remainder - second_step * direction[:, columns]
-        return carry
-
-    lax.fori_loop(0, blocks, output_step, 0)
+    scalars[0:1, :] = jnp.broadcast_to(first_step, (1, LANES))
+    scalars[1:2, :] = jnp.broadcast_to(ratio, (1, LANES))
+    scalars[2:8, :] = jnp.broadcast_to(second_step, (6, LANES))
 
 
 def per_device(loads, coords, coreg_factor, noise, run_perm, block_nbrs, nbr_count):
@@ -500,11 +511,11 @@
     smem = pl.BlockSpec(memory_space=pltpu.SMEM)
     wide = pltpu.VMEM((rows, runs), F32)
     wide_out = jax.ShapeDtypeStruct((rows, runs), F32)
-    return pl.pallas_call(
+    image, second_image, scalars = pl.pallas_call(
         functools.partial(solver, samp_count, blocks, slots),
-        out_shape=[wide_out, wide_out],
+        out_shape=[wide_out, wide_out, jax.ShapeDtypeStruct((8, LANES), F32)],
         in_specs=[vmem] * 5 + [smem] * 2,
-        out_specs=[vmem] * 2,
+        out_specs=[vmem] * 3,
         scratch_shapes=[
             pltpu.VMEM((3 * (rows + 8), runs), BF16),
             pltpu.VMEM((2 * rows, runs), BF16),
@@ -512,7 +523,6 @@
             pltpu.VMEM((runs // 6, 2 * LANES), jnp.int32),
             pltpu.VMEM((1, runs), jnp.int32),
             pltpu.VMEM((runs, LANES), F32),
-            wide,
             pltpu.VMEM((8, extent), F32),
             pltpu.VMEM((LANES, runs), BF16),
             pltpu.VMEM((extent // LANES, LANES, LANES), BF16),
@@ -523,14 +533,14 @@
             pltpu.VMEM((2, chans, rows, runs), BF16),
             pltpu.VMEM((extent // LANES, rows, LANES), BF16),
             pltpu.VMEM((extent // LANES, rows, LANES), BF16),
-            pltpu.VMEM((2, chans, 24, LANES), F32),
-            pltpu.VMEM((2, samp_count, 24, LANES), F32),
+            pltpu.VMEM((2, chans, 8, LANES), F32),
+            pltpu.VMEM((2, samp_count, 8, LANES), F32),
             pltpu.SemaphoreType.DMA((3,)),
             pltpu.SemaphoreType.DMA((3,)),
             pltpu.SemaphoreType.DMA((2, 3, CHUNKS)),
             pltpu.SemaphoreType.DMA((2, 3, CHUNKS)),
-            pltpu.SemaphoreType.DMA((3, 2)),
-            pltpu.SemaphoreType.DMA((3, 2)),
+            pltpu.SemaphoreType.DMA((3, 2, CHUNKS)),
+            pltpu.SemaphoreType.DMA((3, 2, CHUNKS)),
             pltpu.SemaphoreType.DMA((2, 3)),
             pltpu.SemaphoreType.DMA((2, 3)),
             pltpu.SemaphoreType.DMA((2, samp_count)),
@@ -545,9 +555,13 @@
         coreg_factor,
         noise[None, :],
         run_perm[None, :],
-        block_nbrs,
+        block_nbrs.T,
         nbr_count,
     )
+    first_step, ratio, second_step = scalars[0, 0], scalars[1, 0], scalars[2, 0]
+    remainder = loads - first_step * image
+    step = remainder + ratio * loads
+    return first_step * loads + second_step * step, remainder - second_step * second_image
 
 
 def solution(mesh):

time: 97.8 us -> 85.4 us (0.87)
  Pallas kernels: 92.6 us -> 78.5 us
  other arithmetic: 0 us -> 4.68 us
  local copies, waits for them, and re-layouts: 4.4 us -> 1.39 us
    pallas_call x1, Pallas kernels: 92.6 us -> 78.5 us  [per_device(): pl.pallas_call(functools.partial(solver, samp_count, blocks, slots), out_...]
    sub x0 -> x1, other arithmetic: none -> 4.68 us  [per_device(): remainder - second_step * second_image]
    unnamed x5 -> x2, local copies, waits for them, and re-layouts: 4.4 us -> 0.01 us
    slice x0 -> x1, local copies, waits for them, and re-layouts: none -> 1.38 us  [per_device(): scalars[0, 0]]
where the time goes in v3:
time: 85.4 us; the launch traced here: 85.2 us
  Pallas kernels  78.5 us (92%)
  other arithmetic  4.68 us (5%)
  local copies, waits for them, and re-layouts  1.39 us (2%)
    pallas_call x1, Pallas kernels, per_device(): pl.pallas_call(functools.partial(solver, samp_count, blocks, slots), out_...  78.5 us
    sub x1, other arithmetic, per_device(): remainder - second_step * second_image  4.68 us

profile of v3, /device:TPU:0, one launch (start us, length us, event | category | flops | bytes accessed | tf_op | source)
XLA Modules:
  0.0 85.2 jit_solution(10549907367112638098)
XLA Ops:
  0.6 0.0 copy-start
  0.6 78.5 %shard_map.86 = (f32[64,3072]{1,0:T(8,128)}, f32[64,3072]{1,0:T(8,128)}, f32[8,128]{1,0:T(8,128)}) custom-call(f32[64,3072]{1,0:T(8,128)} %loads.1, f32[6,3072]{1,0:T(8,128)} %coords.1, f32[64,256]{1,0:T(8,128)} %factor.1, f32[1,64]{1,0:T(1,128)} %bitcast.8, s32[1,3072]{1,0:T(1,128)} %bitcast.6, s32[12,24]{1,0:T(8,128)} %bitcast.7, s32[24]{0:T(128)} %counts.1), custom_call_target="tpu_custom_call" | custom-call | tf_op jit(solution)/shard_map/pallas_call | solution.py:514
  79.1 1.4 %fusion = (f32[1,1]{1,0:T(1,128)}, f32[1,1]{1,0:T(1,128)}, f32[1,1]{1,0:T(1,128)}) fusion(f32[8,128]{1,0:T(8,128)} %get-tuple-element.5), kind=kLoop, calls=%fused_computation.3 | loop fusion | bytes 24 | tf_op jit(solution)/shard_map/slice | solution.py:561
  80.5 0.0 copy-done
  80.5 4.7 %multiply_subtract_fusion = (f32[64,3072]{1,0:T(8,128)}, f32[64,3072]{1,0:T(8,128)}) fusion(f32[64,3072]{1,0:T(8,128)} %get-tuple-element.7, f32[64,3072]{1,0:T(8,128)S(1)} %copy-done, f32[64,3072]{1,0:T(8,128)} %get-tuple-element.6, f32[]{:T(128)} %bitcast.4, f32[]{:T(128)} %bitcast.3, f32[]{:T(128)} %bitcast.5), kind=kLoop, calls=%fused_computation | loop fusion | flops 1769472 | bytes 3932172 | tf_op jit(solution)/shard_map/sub | solution.py:564
Async XLA Ops:
  0.6 79.9 %copy-start = (f32[64,3072]{1,0:T(8,128)S(1)}, f32[64,3072]{1,0:T(8,128)}, u32[]{:S(2)}) copy-start(f32[64,3072]{1,0:T(8,128)} %loads.1) | copy-start | bytes 2359300

commit v4 on v3

--- a/solution.py
+++ b/solution.py
@@ -87,7 +87,7 @@
                 axis=0,
             )
         )
-        source[:, columns] = jnp.concatenate(parts, axis=0).astype(BF16)
+        source[:, columns] = jnp.concatenate(parts[:2], axis=0).astype(BF16)
     depth = runs // 6
     for begin in range(0, depth, LANES):
         position[begin : begin + LANES, :] = (
@@ -97,7 +97,7 @@
     def sort_step(pair, carry):
         columns = pl.ds(pl.multiple_of(pair * stride, stride), stride)
         target = perm_rows[:, columns]
-        total = jnp.zeros((3 * (rows + 8), stride), F32)
+        total = jnp.zeros((2 * (rows + 8), stride), F32)
         for part in range(6):
             chosen = jnp.where(position[...] == target - part * depth, 1.0, 0.0).astype(BF16)
             total = total + jnp.dot(
@@ -105,8 +105,7 @@
                 chosen,
                 preferred_element_type=F32,
             )
-        high, middle, low = (total[n * (rows + 8) : (n + 1) * (rows + 8)] for n in range(3))
-        result = high + middle + low
+        result = total[0 : rows + 8] + total[rows + 8 :]
         sorted_loads[:, columns] = result[0:rows]
         coords_ext[:, pl.ds(pl.multiple_of(halo + pair * stride, LANES), stride)] = result[rows:]
         return carry
@@ -298,7 +297,6 @@
         return carry
 
     lax.fori_loop(0, blocks, own_step, 0)
-    halo_wait(coord_copies)
 
     def ext_step(tile, carry):
         point = coords_ext[:, lane_tile(tile)]
@@ -311,7 +309,22 @@
         ext_terms[tile] = stacked.T.astype(BF16)
         return carry
 
-    lax.fori_loop(0, extent // LANES, ext_step, 0)
+    lax.fori_loop(edge, edge + blocks, ext_step, 0)
+    lax.fori_loop(0, blocks, column_step, 0)
+    for copy in factor_copies:
+        copy.wait()
+    coreg_rows = lax.dot_general(
+        factor[...],
+        factors[...].reshape(4 * rows, factor.shape[1]),
+        (((1,), (1,)), ((), ())),
+        precision=lax.Precision.HIGHEST,
+        preferred_element_type=F32,
+    )
+    for number, piece in enumerate(pieces(coreg_rows)):
+        coreg[number * rows : (number + 1) * rows, :] = piece.astype(BF16)
+    halo_wait(coord_copies)
+    lax.fori_loop(0, edge, ext_step, 0)
+    lax.fori_loop(edge + blocks, widened, ext_step, 0)
 
     def window_start(block):
         return jnp.clip(nbrs[0, block] - samp * blocks + edge, 0, widened - slots)
@@ -332,18 +345,6 @@
             tiles[block, slot * LANES : (slot + 1) * LANES, :] = tile.astype(BF16)
         return carry
 
-    for copy in factor_copies:
-        copy.wait()
-    coreg_rows = lax.dot_general(
-        factor[...],
-        factors[...].reshape(4 * rows, factor.shape[1]),
-        (((1,), (1,)), ((), ())),
-        precision=lax.Precision.HIGHEST,
-        preferred_element_type=F32,
-    )
-    for number, piece in enumerate(pieces(coreg_rows)):
-        coreg[number * rows : (number + 1) * rows, :] = piece.astype(BF16)
-
     def mix(turn, part):
         gather_finish(turn, part)
         for begin in range(part * chunk, (part + 1) * chunk, stride):
@@ -451,7 +452,9 @@
 
     sums = lax.fori_loop(0, blocks, first_apply, (nothing, nothing, nothing))
     reduce_begin(0, sums)
+    unsort_begin(image)
     reduce_middle(0)
+    unsort(image_out, 0, pairs)
     norm_now, dot, square = reduce_end(0)
     first_step = norm_now / dot
     norm_next = jnp.maximum(
@@ -471,11 +474,10 @@
             gathered[1, chan, :, columns] = step.astype(BF16)
         gather_start(1, part)
 
-    lax.fori_loop(0, blocks, column_step, 0)
-    unsort_begin(image)
     copies = []
     for part in range(CHUNKS):
-        unsort(image_out, part * pairs, (part + 1) * pairs)
+        if part:
+            unsort(image_out, part * pairs, (part + 1) * pairs)
         gather_forward(1, part)
         if part:
             copies.append(mix(1, part - 1))
@@ -490,14 +492,23 @@
 
     dot_sum = lax.fori_loop(0, blocks, second_apply, nothing)
     reduce_begin(1, [norm_sum, dot_sum])
+    unsort_begin(image)
     reduce_middle(1)
-    unsort_begin(image)
     unsort(second_out, 0, runs // stride)
     norm_last, dot_last, _ = reduce_end(1)
     second_step = norm_last / dot_last
     scalars[0:1, :] = jnp.broadcast_to(first_step, (1, LANES))
     scalars[1:2, :] = jnp.broadcast_to(ratio, (1, LANES))
     scalars[2:8, :] = jnp.broadcast_to(second_step, (6, LANES))
+
+
+def finisher(loads, image, second_image, scalars, sol, res):
+    first_step, ratio, second_step = (scalars[row : row + 1, 0:1] for row in range(3))
+    right = loads[...]
+    remainder = right - first_step * image[...]
+    step = remainder + ratio * right
+    sol[...] = first_step * right + second_step * step
+    res[...] = remainder - second_step * second_image[...]
 
 
 def per_device(loads, coords, coreg_factor, noise, run_perm, block_nbrs, nbr_count):
@@ -517,7 +528,7 @@
         in_specs=[vmem] * 5 + [smem] * 2,
         out_specs=[vmem] * 3,
         scratch_shapes=[
-            pltpu.VMEM((3 * (rows + 8), runs), BF16),
+            pltpu.VMEM((2 * (rows + 8), runs), BF16),
             pltpu.VMEM((2 * rows, runs), BF16),
             wide,
             pltpu.VMEM((runs // 6, 2 * LANES), jnp.int32),
@@ -558,10 +569,15 @@
         block_nbrs.T,
         nbr_count,
     )
-    first_step, ratio, second_step = scalars[0, 0], scalars[1, 0], scalars[2, 0]
-    remainder = loads - first_step * image
-    step = remainder + ratio * loads
-    return first_step * loads + second_step * step, remainder - second_step * second_image
+    block = pl.BlockSpec((rows // 4, runs), lambda step: (step, 0))
+    return pl.pallas_call(
+        finisher,
+        grid=(4,),
+        out_shape=[wide_out, wide_out],
+        in_specs=[block] * 3 + [pl.BlockSpec((8, LANES), lambda step: (0, 0))],
+        out_specs=[block] * 2,
+        compiler_params=pltpu.CompilerParams(vmem_limit_bytes=60 * 2**20),
+    )(loads, image, second_image, scalars)
 
 
 def solution(mesh):

time: 85.4 us -> 82 us (0.960)
  other arithmetic: 4.68 us -> 0 us
  Pallas kernels: 78.5 us -> 81.2 us
  local copies, waits for them, and re-layouts: 1.39 us -> 0 us
    sub x1 -> x0, other arithmetic: 4.68 us -> none  [per_device(): remainder - second_step * second_image]
    pallas_call x0 -> x1, Pallas kernels: none -> 3.92 us  [per_device(): pl.pallas_call(finisher, grid=(4,), out_shape=[wide_out, wide_out], in_sp...]
    slice x1 -> x0, local copies, waits for them, and re-layouts: 1.38 us -> none  [per_device(): scalars[0, 0]]
    pallas_call x1, Pallas kernels: 78.5 us -> 77.3 us  [per_device(): pl.pallas_call(functools.partial(solver, samp_count, blocks, slots), out_...]
where the time goes in v4:
time: 82 us; the launch traced here: 81.8 us
  Pallas kernels  81.2 us (99%)
    pallas_call x1, Pallas kernels, per_device(): pl.pallas_call(functools.partial(solver, samp_count, blocks, slots), out_...  77.3 us
    pallas_call x1, Pallas kernels, per_device(): pl.pallas_call(finisher, grid=(4,), out_shape=[wide_out, wide_out], in_sp...  3.92 us

profile of v4, /device:TPU:0, one launch (start us, length us, event | category | flops | bytes accessed | tf_op | source)
XLA Modules:
  0.0 81.8 jit_solution(14879385425431791504)
XLA Ops:
  0.6 77.3 %shard_map.86 = (f32[64,3072]{1,0:T(8,128)}, f32[64,3072]{1,0:T(8,128)}, f32[8,128]{1,0:T(8,128)}) custom-call(f32[64,3072]{1,0:T(8,128)} %loads.3, f32[6,3072]{1,0:T(8,128)} %coords.1, f32[64,256]{1,0:T(8,128)} %factor.1, f32[1,64]{1,0:T(1,128)} %bitcast.5, s32[1,3072]{1,0:T(1,128)} %bitcast.3, s32[12,24]{1,0:T(8,128)} %bitcast.4, s32[24]{0:T(128)} %counts.1), custom_call_target="tpu_custom_call" | custom-call | tf_op jit(solution)/shard_map/pallas_call | solution.py:525
  77.9 3.9 %shard_map.87 = (f32[64,3072]{1,0:T(8,128)}, f32[64,3072]{1,0:T(8,128)}) custom-call(f32[64,3072]{1,0:T(8,128)} %loads.3, f32[64,3072]{1,0:T(8,128)} %get-tuple-element.5.image, f32[64,3072]{1,0:T(8,128)} %get-tuple-element.6.second_image, f32[8,128]{1,0:T(8,128)} %get-tuple-element.7.scalars), custom_call_target="tpu_custom_call" | custom-call | tf_op jit(solution)/shard_map/pallas_call | solution.py:573

commit v5 on v4

--- a/solution.py
+++ b/solution.py
@@ -450,7 +450,7 @@
         image[:, lane_tile(block)] = mapped
         return norm + operand * operand, dot + operand * mapped, square + mapped * mapped
 
-    sums = lax.fori_loop(0, blocks, first_apply, (nothing, nothing, nothing))
+    sums = lax.fori_loop(0, blocks, first_apply, (nothing, nothing, nothing), unroll=2)
     reduce_begin(0, sums)
     unsort_begin(image)
     reduce_middle(0)
@@ -490,7 +490,7 @@
         image[:, lane_tile(block)] = mapped
         return total + operand * mapped
 
-    dot_sum = lax.fori_loop(0, blocks, second_apply, nothing)
+    dot_sum = lax.fori_loop(0, blocks, second_apply, nothing, unroll=2)
     reduce_begin(1, [norm_sum, dot_sum])
     unsort_begin(image)
     reduce_middle(1)

time: 82 us -> 79 us (0.963)
  Pallas kernels: 81.2 us -> 78.1 us
    pallas_call x1, Pallas kernels: 77.3 us -> 74.2 us  [per_device(): pl.pallas_call(functools.partial(solver, samp_count, blocks, slots), out_...]
where the time goes in v5:
time: 79 us; the launch traced here: 78.8 us
  Pallas kernels  78.1 us (99%)
    pallas_call x1, Pallas kernels, per_device(): pl.pallas_call(functools.partial(solver, samp_count, blocks, slots), out_...  74.2 us
    pallas_call x1, Pallas kernels, per_device(): pl.pallas_call(finisher, grid=(4,), out_shape=[wide_out, wide_out], in_sp...  3.92 us

profile of v5, /device:TPU:0, one launch (start us, length us, event | category | flops | bytes accessed | tf_op | source)
XLA Modules:
  0.0 78.8 jit_solution(9673810959205550170)
XLA Ops:
  0.6 74.2 %shard_map.86 = (f32[64,3072]{1,0:T(8,128)}, f32[64,3072]{1,0:T(8,128)}, f32[8,128]{1,0:T(8,128)}) custom-call(f32[64,3072]{1,0:T(8,128)} %loads.3, f32[6,3072]{1,0:T(8,128)} %coords.1, f32[64,256]{1,0:T(8,128)} %factor.1, f32[1,64]{1,0:T(1,128)} %bitcast.5, s32[1,3072]{1,0:T(1,128)} %bitcast.3, s32[12,24]{1,0:T(8,128)} %bitcast.4, s32[24]{0:T(128)} %counts.1), custom_call_target="tpu_custom_call" | custom-call | tf_op jit(solution)/shard_map/pallas_call | solution.py:525
  74.8 3.9 %shard_map.87 = (f32[64,3072]{1,0:T(8,128)}, f32[64,3072]{1,0:T(8,128)}) custom-call(f32[64,3072]{1,0:T(8,128)} %loads.3, f32[64,3072]{1,0:T(8,128)} %get-tuple-element.5.image, f32[64,3072]{1,0:T(8,128)} %get-tuple-element.6.second_image, f32[8,128]{1,0:T(8,128)} %get-tuple-element.7.scalars), custom_call_target="tpu_custom_call" | custom-call | tf_op jit(solution)/shard_map/pallas_call | solution.py:573

commit v6 on v5

--- a/solution.py
+++ b/solution.py
@@ -450,7 +450,7 @@
         image[:, lane_tile(block)] = mapped
         return norm + operand * operand, dot + operand * mapped, square + mapped * mapped
 
-    sums = lax.fori_loop(0, blocks, first_apply, (nothing, nothing, nothing), unroll=2)
+    sums = lax.fori_loop(0, blocks, first_apply, (nothing, nothing, nothing), unroll=4)
     reduce_begin(0, sums)
     unsort_begin(image)
     reduce_middle(0)
@@ -490,7 +490,7 @@
         image[:, lane_tile(block)] = mapped
         return total + operand * mapped
 
-    dot_sum = lax.fori_loop(0, blocks, second_apply, nothing, unroll=2)
+    dot_sum = lax.fori_loop(0, blocks, second_apply, nothing, unroll=4)
     reduce_begin(1, [norm_sum, dot_sum])
     unsort_begin(image)
     reduce_middle(1)

time: 79 us -> 77.4 us (0.980)
  Pallas kernels: 78.1 us -> 76.6 us
    pallas_call x1, Pallas kernels: 74.2 us -> 72.6 us  [per_device(): pl.pallas_call(functools.partial(solver, samp_count, blocks, slots), out_...]
where the time goes in v6:
time: 77.4 us; the launch traced here: 77.2 us
  Pallas kernels  76.6 us (99%)
    pallas_call x1, Pallas kernels, per_device(): pl.pallas_call(functools.partial(solver, samp_count, blocks, slots), out_...  72.6 us
    pallas_call x1, Pallas kernels, per_device(): pl.pallas_call(finisher, grid=(4,), out_shape=[wide_out, wide_out], in_sp...  3.92 us

profile of v6, /device:TPU:0, one launch (start us, length us, event | category | flops | bytes accessed | tf_op | source)
XLA Modules:
  0.0 77.2 jit_solution(4631997397859517581)
XLA Ops:
  0.6 72.6 %shard_map.86 = (f32[64,3072]{1,0:T(8,128)}, f32[64,3072]{1,0:T(8,128)}, f32[8,128]{1,0:T(8,128)}) custom-call(f32[64,3072]{1,0:T(8,128)} %loads.3, f32[6,3072]{1,0:T(8,128)} %coords.1, f32[64,256]{1,0:T(8,128)} %factor.1, f32[1,64]{1,0:T(1,128)} %bitcast.5, s32[1,3072]{1,0:T(1,128)} %bitcast.3, s32[12,24]{1,0:T(8,128)} %bitcast.4, s32[24]{0:T(128)} %counts.1), custom_call_target="tpu_custom_call" | custom-call | tf_op jit(solution)/shard_map/pallas_call | solution.py:525
  73.3 3.9 %shard_map.87 = (f32[64,3072]{1,0:T(8,128)}, f32[64,3072]{1,0:T(8,128)}) custom-call(f32[64,3072]{1,0:T(8,128)} %loads.3, f32[64,3072]{1,0:T(8,128)} %get-tuple-element.5.image, f32[64,3072]{1,0:T(8,128)} %get-tuple-element.6.second_image, f32[8,128]{1,0:T(8,128)} %get-tuple-element.7.scalars), custom_call_target="tpu_custom_call" | custom-call | tf_op jit(solution)/shard_map/pallas_call | solution.py:573
